TPU v7x, 512 devices: a whole 4x8x8 slice. The times are simulated.
512 devices in a mesh: dp: 8 (over x, core), ctx: 64 (over z, y).
Axes of the slice: x: 4, y: 8, z: 8, core: 2. Of those that a mesh axis runs over, the one named last changes fastest.
Arguments:
- query: bfloat16 [32768, 2048], P('ctx', 'dp'), may hold values from -6 to 6
- key_in: bfloat16 [32768, 2048], P('ctx', 'dp'), may hold values from -6 to 6
- value: bfloat16 [32768, 2048], P('ctx', 'dp'), may hold values from -6 to 6
- latent: bfloat16 [32768, 16], P('ctx'), may hold values from -24 to 24
- w_b: bfloat16 [16, 2048], P(None, 'dp'), may hold values from -1.5 to 1.5
- gate_bias: float32 [2048], P('dp'), may hold values from -1 to 10
- doc_ids: int32 [32768], P('ctx'), may hold values from 0 to 31, as said below
- d_out: bfloat16 [32768, 2048], P('ctx', 'dp'), may hold values from -6 to 6
Outputs:
- output: bfloat16 [32768, 2048], P('ctx', 'dp')
- grad_query: bfloat16 [32768, 2048], P('ctx', 'dp')
- sensitivity_addresses: bfloat16 [32768, 2048], P('ctx', 'dp')
- grad_value: bfloat16 [32768, 2048], P('ctx', 'dp')
- grad_latent: float32 [32768, 16], P('ctx')
- grad_w_b: float32 [16, 2048], P(None, 'dp')
- grad_gate_bias: float32 [2048], P('dp')
Inputs may be any that keep to these rules, and one draw needn't show every extreme that they name: doc_ids never fall and number 32 documents; a document holds 1 to 3072 positions; the first holds exactly 3072.
All inputs are finite; a program needn't handle non-finite values.
Results may differ from a plain program's by a relative error of at most 0.0013.
Values sent between devices are 32-bit elements; how exact they have to be, the bound alone decides.
No kernel may reach another device: no remote copies, remote signals or barrier semaphores. Data moves between devices by JAX's collectives and lax.ppermute only.
A program may use at most 64 MiB of HBM per device.

v0:
```python
import jax
import jax.numpy as jnp
from jax import lax
from jax.sharding import PartitionSpec as P

HEAD = 128
GROUP = 64


precise_mode = lax.Precision.HIGHEST


def prefix(part, axis, combine, identity, reverse):
    count = lax.axis_size(axis)
    place = lax.axis_index(axis)
    ahead = count - 1 - place if reverse else place
    gathered = jax.tree.map(lambda a: lax.all_gather(a, axis), part)
    state = jax.tree.map(lambda a, e: jnp.zeros_like(a) + jnp.asarray(e, a.dtype), part, identity)

    def one(lap, state):
        source = count - 1 - lap if reverse else lap
        return combine(
            state, jax.tree.map(lambda a: lax.dynamic_index_in_dim(a, source, 0, False), gathered)
        )

    return lax.fori_loop(0, ahead, one, state)


def passed_along(value, axis, steps):
    count = lax.axis_size(axis)
    initial, last = (max(0, -steps), min(count, count - steps))
    return lax.ppermute(value, axis, [(source, source + steps) for source in range(initial, last)])


def group_pass(carried_in, pieces):
    memory_state, prev_id = carried_in
    queries, address_share, values_portion, log_gate, segment = pieces
    decay_sum = jnp.cumsum(log_gate, axis=0)
    positions = jnp.arange(segment.shape[0])
    visible = (positions[:, None] >= positions[None, :]) & (segment[:, None] == segment[None, :])
    query_decay = queries * jnp.exp(decay_sum)
    k_decay = address_share * jnp.exp(-decay_sum)
    scores = jnp.einsum("ihk,jhk->hij", query_decay, k_decay, precision=precise_mode)
    scores = jnp.where(visible[None], scores, 0.0)
    inner = jnp.einsum("hij,jhv->ihv", scores, values_portion, precision=precise_mode)
    leading_mask = (segment == prev_id).astype(jnp.float32)
    outer_product = leading_mask[:, None, None] * jnp.einsum(
        "scd,cdx->scx", query_decay, memory_state, precision=precise_mode
    )
    result = (inner + outer_product) * HEAD ** (-0.5)
    last_id = segment[-1]
    total_decay = decay_sum[-1]
    tail_mask = (segment == last_id).astype(jnp.float32)
    key_tail_decay = (
        address_share * jnp.exp(total_decay[None] - decay_sum) * tail_mask[:, None, None]
    )
    keep_state_flag = (last_id == prev_id).astype(jnp.float32)
    memory_state = keep_state_flag * jnp.exp(total_decay)[:, :, None] * memory_state + jnp.einsum(
        "upw,upl->pwl", key_tail_decay, values_portion, precision=precise_mode
    )
    return ((memory_state, last_id), result)


def gate_logs(latent_part, weight_part, bias_part):
    gate_pre = jnp.dot(latent_part, weight_part, precision=precise_mode) + bias_part
    return jnp.maximum(jax.nn.log_sigmoid(gate_pre) / 16.0, -0.5)


def device_pass(queries, address_share, values_portion, log_gate, segment, prev_id, memory_in):
    pieces = tuple(
        (
            source.reshape((-1, GROUP) + source.shape[1:])
            for source in (queries, address_share, values_portion, log_gate)
        )
    )
    (memory_state, last_id), result = lax.scan(
        group_pass, (memory_in, prev_id), pieces + (segment.reshape(-1, GROUP),)
    )
    return (result.reshape(queries.shape), memory_state)


def affine_combine(earlier, later_pair):
    return (earlier[0] * later_pair[0], later_pair[1] + later_pair[0][..., None] * earlier[1])


def chain_prefix(affine_pair, reverse):
    identity = (jnp.ones_like(affine_pair[0]), jnp.zeros_like(affine_pair[1]))
    return prefix(affine_pair, "ctx", affine_combine, identity, reverse)


def body(query, key_in, value, latent, w_b, gate_bias, doc_ids, d_out):
    tokens = query.shape[0]
    head_shape = (tokens, query.shape[1] // HEAD, HEAD)
    queries = query.astype(jnp.float32).reshape(head_shape)
    key_rows = key_in.astype(jnp.float32).reshape(head_shape)
    value_matrix_rows = value.astype(jnp.float32).reshape(head_shape)
    gradient_rows = d_out.astype(jnp.float32).reshape(head_shape)

    def gate_shaped(latent_part, weight_part, bias_part):
        return gate_logs(latent_part, weight_part, bias_part).reshape(head_shape)

    log_gate, gate_pullback = jax.vjp(
        gate_shaped, latent.astype(jnp.float32), w_b.astype(jnp.float32), gate_bias
    )
    neighbor_id = passed_along(doc_ids[-1:] + 1, "ctx", 1)[0]
    prev_id = neighbor_id - 1
    decay_sum = jnp.cumsum(log_gate, axis=0)
    total_decay = decay_sum[-1]
    through = jnp.all(doc_ids == prev_id)
    factor = jnp.where(through, jnp.exp(total_decay), 0.0)
    tail_mask = (doc_ids == doc_ids[-1]).astype(jnp.float32)
    key_tail_decay = key_rows * jnp.exp(total_decay[None] - decay_sum) * tail_mask[:, None, None]
    carried_state = jnp.einsum(
        "upw,upl->pwl", key_tail_decay, value_matrix_rows, precision=precise_mode
    )
    leading_mask = (doc_ids == prev_id).astype(jnp.float32)
    query_leading = queries * jnp.exp(decay_sum) * (leading_mask[:, None, None] * HEAD ** (-0.5))
    pulled_gradient = jnp.einsum(
        "qgm,qgd->gmd", query_leading, gradient_rows, precision=precise_mode
    )
    memory_in = chain_prefix((factor, carried_state), False)[1]
    memory_back = chain_prefix((factor, pulled_gradient), True)[1]

    def local_pass(query_part, key_part, value_part, gate_part, memory_part):
        return device_pass(
            query_part, key_part, value_part, gate_part, doc_ids, prev_id, memory_part
        )

    (result, memory_out), pullback = jax.vjp(
        local_pass, queries, key_rows, value_matrix_rows, log_gate, memory_in
    )
    grad_query, sensitivity_addresses, grad_value, grad_gate, _ = pullback(
        (gradient_rows, memory_back)
    )
    grad_latent, grad_weight, grad_bias = gate_pullback(grad_gate)
    grad_latent = lax.psum(grad_latent, "dp")
    grad_weight, grad_bias = lax.psum((grad_weight, grad_bias), "ctx")
    flat_shape = (tokens, query.shape[1])
    return (
        result.reshape(flat_shape).astype(jnp.bfloat16),
        grad_query.reshape(flat_shape).astype(jnp.bfloat16),
        sensitivity_addresses.reshape(flat_shape).astype(jnp.bfloat16),
        grad_value.reshape(flat_shape).astype(jnp.bfloat16),
        grad_latent,
        grad_weight,
        grad_bias,
    )


def solution(mesh):
    in_specs = (
        P("ctx", "dp"),
        P("ctx", "dp"),
        P("ctx", "dp"),
        P("ctx", None),
        P(None, "dp"),
        P("dp"),
        P("ctx"),
        P("ctx", "dp"),
    )
    out_specs = (
        P("ctx", "dp"),
        P("ctx", "dp"),
        P("ctx", "dp"),
        P("ctx", "dp"),
        P("ctx", None),
        P(None, "dp"),
        P("dp"),
    )
    return jax.shard_map(body, mesh=mesh, in_specs=in_specs, out_specs=out_specs, check_vma=False)
```

profile of v0, /device:TPU:6, one launch (start us, length us, event | category | flops | bytes accessed | tf_op | source)
XLA Modules:
  0.0 823.5 jit_solution(7295074931941470318)
XLA Ops:
  9.2 4.8 collective-permute-start
  15.4 2.1 fusion.89
  18.2 1.3 compare_convert_fusion.4
  23.0 3.9 multiply_multiply_fusion.1
  26.9 2.2 fusion.80
  32.0 2.0 reshape.290
  34.9 55.4 %all_gather.20 = f32[64,2,128]{2,1,0:T(2,128)S(1)} all-gather(f32[1,2,128]{2,1,0:T(2,128)} %get-tuple-element.1351), channel_id=1, replica_groups=mesh['dp'=8,'ctx'=64] {'ctx'}, dimensions={0}, use_global_device_ids=true | all-gather | bytes 66560 | tf_op jit(solution)/shard_map/all_gather | solution.py:17
  90.2 42.2 %all-gather.7.cloned.1.call-done = f32[128,128,128]{2,1,0:T(8,128)} async-done(((f32[2,128,128]{2,1,0:T(8,128)}), f32[128,128,128]{2,1,0:T(8,128)}) %all-gather.7.cloned.1.call-update) | async-done | bytes 8388624 | tf_op jit(solution)/shard_map/all_gather | solution.py:17
  132.4 67.4 %while.93 = (s32[]{:T(128)}, f32[2,128,128]{2,1,0:T(8,128)S(1)}, s32[]{:T(128)}, f32[64,2,128,128]{3,2,1,0:T(8,128)}, f32[64,2,128]{2,1,0:T(2,128)S(1)}, /*index=5*/s32[]{:T(128)}, s32[]{:T(128)}, s32[]{:T(128)}, s32[]{:T(128)}) while((s32[]{:T(128)}, f32[2,128,128]{2,1,0:T(8,128)S(1)}, s32[]{:T(128)}, f32[64,2,128,128]{3,2,1,0:T(8,128)}, ...), condition=%wide.region_9.10_spmd, body=%wide.region_8.9_spmd.sunk | while | flops 65542 | bytes 396443 | solution.py:26
  199.8 33.7 %all-gather.5.cloned.1.call-done = f32[128,128,128]{2,1,0:T(8,128)} async-done(((f32[2,128,128]{2,1,0:T(8,128)}), f32[128,128,128]{2,1,0:T(8,128)}) %all-gather.5.cloned.1.call-update) | async-done | bytes 8388624 | tf_op jit(solution)/shard_map/all_gather | solution.py:17
  238.8 91.7 %while.95 = (s32[]{:T(128)}, f32[2,128,128]{2,1,0:T(8,128)S(1)}, s32[]{:T(128)}, bf16[8,64,2,128]{3,1,2,0:T(8,128)(2,1)S(1)}, f32[8,64,2,128]{3,2,1,0:T(2,128)},...) while((s32[]{:T(128)}, f32[2,128,128]{2,1,0:T(8,128)S(1)}, ...), condition=%wide.region_7.8_spmd.clone, body=%wide.region_5.7_spmd.clone.sunk | while | flops 76862464 | bytes 2567755 | solution.py:76
  332.1 108.8 %while.94 = (s32[]{:T(128)}, f32[2,128,128]{2,1,0:T(8,128)S(1)}, bf16[8,64,2,128]{3,1,2,0:T(8,128)(2,1)S(1)}, bf16[8,64,2,128]{3,1,2,0:T(8,128)(2,1)S(1)}, bf16[...) while((s32[]{:T(128)}, f32[2,128,128]{2,1,0:T(8,128)S(1)}, ...), condition=%wide.region_14.15_spmd, body=%wide.region_10.14_spmd.sunk | while | flops 152576320 | bytes 4786497 | solution.py:76
  341.1 1.8 fusion.151
  354.6 1.8 fusion.151
  365.4 1.3 fusion.149
  368.2 1.8 fusion.151
  381.8 1.8 fusion.151
  395.4 1.8 fusion.151
  409.0 1.8 fusion.151
  422.6 1.8 fusion.151
  436.2 1.8 fusion.151
  441.8 1.7 fusion.94
  447.8 22.2 %psum.21 = f32[512,16]{0,1:T(8,128)} all-reduce(f32[512,16]{0,1:T(8,128)S(1)} %fusion.87), channel_id=1, replica_groups=mesh['dp'=8,'ctx'=64] {'dp'}, use_global_device_ids=true, to_apply=%region_15.16 | all-reduce | flops 8192 | bytes 65536 | tf_op jit(solution)/shard_map/psum | solution.py:136
  471.7 344.9 %all-reduce.1 = (f32[16,256]{1,0:T(8,128)}, f32[256]{0:T(256)}) all-reduce(f32[16,256]{1,0:T(8,128)S(1)} %convolution_bitcast_fusion.4, f32[256]{0:T(256)S(1)} %neg.65), channel_id=1, replica_groups=mesh['dp'=8,'ctx'=64] {'ctx'}, use_global_device_ids=true, to_apply=%region_16.17 | all-reduce | flops 4352 | bytes 34816 | tf_op jit(solution)/shard_map/psum | solution.py:137
  (517 shorter events, 262.6 us)
Async XLA Ops:
  7.2 8.2 copy-start
  7.2 13.9 %copy-start.6 = (s32[512]{0:T(512)S(1)}, s32[512]{0:T(512)}, u32[]{:S(2)}) copy-start(s32[512]{0:T(512)} %param.22) | copy-start | bytes 6148
  7.2 12.3 %copy-start.5 = (bf16[512,256]{1,0:T(8,128)(2,1)S(1)}, bf16[512,256]{1,0:T(8,128)(2,1)}, u32[]{:S(2)}) copy-start(bf16[512,256]{1,0:T(8,128)(2,1)} %param.17) | copy-start | bytes 786436
  7.2 22.0 %copy-start.1 = (bf16[512,256]{1,0:T(8,128)(2,1)S(1)}, bf16[512,256]{1,0:T(8,128)(2,1)}, u32[]{:S(2)}) copy-start(bf16[512,256]{1,0:T(8,128)(2,1)} %param.18) | copy-start | bytes 786436
  7.2 125.2 %all-gather.7.cloned.1.call-start = ((), (), s32[]{:S(2)}) async-start(), calls=%async_computation.1 | async-start | bytes 8519680 | tf_op jit(solution)/shard_map/all_gather | solution.py:17
  9.2 11.2 %collective-permute-start = (s32[1]{0:T(128)}, s32[1]{0:T(128)}, u32[]{:S(2)}, u32[]{:S(2)}) collective-permute-start(s32[1]{0:T(128)} %add.99), channel_id=1, source_target_pairs={{0,1},{1,2},{2,3},{3,4},{4,5},{5,6},{6,7},{7,8},{8,9},{9,10},{10,1... | collective-permute-start | bytes 20 | tf_op jit(solution)/shard_map/ppermute | solution.py:32
  29.1 204.4 %all-gather.5.cloned.1.call-start = ((), (), s32[]{:S(2)}) async-start(), calls=%async_computation | async-start | bytes 8519680 | tf_op jit(solution)/shard_map/all_gather | solution.py:17
  330.4 0.7 copy-start.2
  332.0 113.1 %copy-start.3 = (bf16[8,64,2,128]{3,1,2,0:T(8,128)(2,1)S(1)}, bf16[8,64,2,128]{3,1,2,0:T(8,128)(2,1)}, u32[]{:S(2)}) copy-start(bf16[8,64,2,128]{3,1,2,0:T(8,128)(2,1)} %copy-done.2) | copy-start | bytes 786436
  440.8 0.7 copy-start.4
Sparse Core Ops, SparseCore 0:
  29.3 103.0 all-gather.6
  136.0 97.4 all-gather.4
where the time goes:
time: 830 us; the launch traced here: 823 us
  blocking collectives  422 us (51%)
  other arithmetic  134 us (16%)
  local copies, waits for them, and re-layouts  91.7 us (11%)
  waiting for transfers between devices  75.9 us (9%)
  matrix products  65.4 us (8%)
  between operations  15.8 us (2%)
  loops' own time  13.7 us (2%)
    psum x1, blocking collectives, body(): grad_weight, grad_bias = lax.psum((grad_weight, grad_bias), 'ctx')  345 us
    all_gather x2, waiting for transfers between devices, prefix(): gathered = jax.tree.map(lambda a: lax.all_gather(a, axis), part)  75.9 us
    add x63, other arithmetic, affine_combine(): later_pair[1] + later_pair[0][..., None] * earlier[1]  64.7 us
    all_gather x1, blocking collectives, prefix(): gathered = jax.tree.map(lambda a: lax.all_gather(a, axis), part)  55.4 us
    dynamic_slice x56, local copies, waits for them, and re-layouts, device_pass(): lax.scan(group_pass, (memory_in, prev_id), pieces + (segment.reshape(-1,...  36.4 us
    dynamic_update_slice x32, other arithmetic, device_pass(): lax.scan(group_pass, (memory_in, prev_id), pieces + (segment.reshape(-1,...  30.9 us
    dynamic_update_slice x32, local copies, waits for them, and re-layouts, device_pass(): lax.scan(group_pass, (memory_in, prev_id), pieces + (segment.reshape(-1,...  24.3 us
    dot_general x24, matrix products, group_pass(): jnp.einsum('hij,jhv->ihv', scores, values_portion, precision=precise_mode)  23.3 us
  transfers between devices with their start and end apart: 3, of which 2 were waited for; matrix products, arithmetic and copies ran while one was open for 9% of the time, Pallas kernels for 0%

commit v1 on v0

v1 whole, which is shorter than its diff:
```python
import jax
import jax.numpy as jnp
from jax import lax
from jax.experimental import pallas as pl
from jax.experimental.pallas import tpu as pltpu
from jax.sharding import Mesh
from jax.sharding import PartitionSpec as P

HEAD = 128
RANK = 16
SPAN = 512
CHUNK = 128
PARTS = SPAN // CHUNK
SCALE = HEAD ** (-0.5)
RING = 8
CTX = ("z", "y")
DP = ("x", "core")

F32 = jnp.float32
BF16 = jnp.bfloat16
NN = (((1,), (0,)), ((), ()))
NT = (((1,), (1,)), ((), ()))
TN = (((0,), (0,)), ((), ()))


def split2(x):
    high = x.astype(BF16)
    return high, (x - high.astype(F32)).astype(BF16)


def split3(x):
    high = x.astype(BF16)
    rest = x - high.astype(F32)
    middle = rest.astype(BF16)
    return high, middle, (rest - middle.astype(F32)).astype(BF16)


def dot(a, b, dims):
    return lax.dot_general(a, b, dims, preferred_element_type=F32)


def dot_left(a, parts, dims):
    (ca,), (cb,) = dims[0]
    return dot(jnp.concatenate([a] * len(parts), axis=ca), jnp.concatenate(parts, axis=cb), dims)


def dot_right(parts, b, dims):
    (ca,), (cb,) = dims[0]
    return dot(jnp.concatenate(parts, axis=ca), jnp.concatenate([b] * len(parts), axis=cb), dims)


def dot_both(a, b, dims):
    (ca,), (cb,) = dims[0]
    left = jnp.concatenate([a[0], a[1], a[0]], axis=ca)
    right = jnp.concatenate([b[0], b[0], b[1]], axis=cb)
    return dot(left, right, dims)


def places():
    rows = lax.broadcasted_iota(jnp.int32, (CHUNK, CHUNK), 0)
    columns = lax.broadcasted_iota(jnp.int32, (CHUNK, CHUNK), 1)
    return rows, columns


def segments(doc_ref, c):
    rows, columns = places()
    row = doc_ref[c : c + 1, :]
    column = jnp.sum(jnp.where(rows == columns, row, 0.0), axis=1, keepdims=True)
    return row, column, row[:, :1], row[:, CHUNK - 1 :]


def as_number(flag):
    return flag.astype(F32)


def state_kernel(
    lat_ref, w_ref, bias_ref, doc_ref, q_ref, k_ref, v_ref, d_ref,
    send_ref, decay_ref, slope_ref, mem_ref, pull_ref,
):
    heads = q_ref.shape[1] // HEAD
    rows, columns = places()
    lower = (rows >= columns).astype(BF16)
    gate_pre = dot(lat_ref[...], w_ref[...], TN) + bias_ref[...]
    small = jnp.exp(-jnp.abs(gate_pre))
    series = small * (1.0 - small * (0.5 - small * (1.0 / 3.0 - small * (0.25 - small * 0.2))))
    log_one = jnp.where(small < 0.02, series, jnp.log(1.0 + small))
    log_gate = -(jnp.maximum(-gate_pre, 0.0) + log_one) / 16.0
    sigmoid = jnp.where(gate_pre >= 0.0, small, 1.0) / (1.0 + small)
    free = jnp.where(log_gate > -0.5, 1.0, jnp.where(log_gate == -0.5, 0.5, 0.0))
    slope_ref[...] = free * sigmoid * (1.0 / 16.0)
    log_gate = jnp.maximum(log_gate, -0.5)
    lower3 = jnp.concatenate([lower] * 3, axis=1)
    for c in range(PARTS):
        at = slice(c * CHUNK, (c + 1) * CHUNK)
        decay_ref[at, :] = dot(lower3, jnp.concatenate(split3(log_gate[at, :]), axis=0), NN)

    seg = [segments(doc_ref, c) for c in range(PARTS)]
    factors = []
    for h in range(heads):
        on = slice(h * HEAD, (h + 1) * HEAD)
        total = None
        memory = None
        pulls, keeps = [], []
        for c in range(PARTS):
            at = slice(c * CHUNK, (c + 1) * CHUNK)
            _, column, first, last = seg[c]
            decay = decay_ref[at, on]
            end = decay[CHUNK - 1 :, :]
            key_tail = k_ref[at, on].astype(F32) * jnp.exp(end - decay) * as_number(column == last)
            added = dot_left(v_ref[at, on], split2(key_tail), TN)
            query_lead = (
                q_ref[at, on].astype(F32) * jnp.exp(decay) * (as_number(column == first) * SCALE)
            )
            pulled = dot_left(d_ref[at, on], split2(query_lead), TN)
            mem_ref[h, c] = added
            pull_ref[h, c] = pulled
            keep = jnp.exp(end) * as_number(first == last)
            keeps.append(keep)
            pulls.append(pulled)
            if c == 0:
                memory, total = added, end
            else:
                memory = added + keep * as_number(first == seg[c - 1][3]) * memory
                total = total + end
        back = pulls[-1]
        for c in reversed(range(PARTS - 1)):
            back = pulls[c] + keeps[c] * as_number(seg[c][3] == seg[c + 1][2]) * back
        whole = jnp.exp(total) * as_number(seg[0][2] == seg[-1][3])
        factors.append(whole)
        each = HEAD // RING
        for j in range(RING):
            send_ref[j, h * each : (h + 1) * each, :] = memory[j * each : (j + 1) * each, :]
            start = heads * each + h * each
            send_ref[j, start : start + each, :] = back[j * each : (j + 1) * each, :]
    ids = [jnp.broadcast_to(seg[0][2] + 1.0, (1, HEAD)), jnp.broadcast_to(seg[-1][3] + 1.0, (1, HEAD))]
    small_rows = jnp.concatenate(factors + ids + [jnp.zeros((4, HEAD), F32)], axis=0)
    for j in range(RING):
        send_ref[j, 64:, :] = small_rows


def taken(got_ref, j):
    factor = jnp.concatenate(
        [jnp.broadcast_to(got_ref[j, 64 + h : 65 + h, :], (16, HEAD)) for h in range(2)], axis=0
    )
    return got_ref[j, 0:32, :], got_ref[j, 32:64, :], factor, got_ref[j, 66:67, :], got_ref[j, 67:68, :]


def total_kernel(got_ref, ahead_ref, behind_ref):
    got = [taken(got_ref, j) for j in range(RING)]
    memory = got[0][0]
    for j in range(1, RING):
        memory = got[j][0] + got[j][2] * as_number(got[j][3] == got[j - 1][4]) * memory
    back = got[-1][1]
    for j in reversed(range(RING - 1)):
        back = got[j][1] + got[j][2] * as_number(got[j][4] == got[j + 1][3]) * back
    zeros = jnp.zeros((7, HEAD), F32)
    ahead_ref[...] = jnp.concatenate([memory, got[-1][4], zeros], axis=0)
    behind_ref[...] = jnp.concatenate([back, got[0][3], zeros], axis=0)


def spread_kernel(got_ref, ahead_ref, behind_ref, send_ref):
    got = [taken(got_ref, j) for j in range(RING)]
    memory = as_number(got[0][3] == ahead_ref[32:33, :]) * ahead_ref[0:32, :]
    for j in range(RING):
        send_ref[j, 0:32, :] = memory
        if j < RING - 1:
            memory = as_number(got[j][4] == got[j + 1][3]) * (got[j][0] + got[j][2] * memory)
    back = as_number(got[-1][4] == behind_ref[32:33, :]) * behind_ref[0:32, :]
    for j in reversed(range(RING)):
        send_ref[j, 32:64, :] = back
        if j > 0:
            back = as_number(got[j - 1][4] == got[j][3]) * (got[j][1] + got[j][2] * back)


def main_kernel(
    lat_ref, w_ref, doc_ref, q_ref, k_ref, v_ref, d_ref, decay_ref, slope_ref, mem_ref, pull_ref,
    got_ref, out_ref, dq_ref, dk_ref, dv_ref, lat_send_ref, w_send_ref,
):
    heads = q_ref.shape[1] // HEAD
    rows, columns = places()
    seg = [segments(doc_ref, c) for c in range(PARTS)]
    earlier = rows >= columns
    masks = [earlier & (seg[c][1] == seg[c][0]) for c in range(PARTS)]
    later = [((columns >= rows) & (seg[c][1] == seg[c][0])).astype(BF16) for c in range(PARTS)]
    grad_lat = None
    grad_w = [None] * heads
    grad_b = [None] * heads
    grad_pre_parts = [[None] * heads for _ in range(PARTS)]
    for h in range(heads):
        on = slice(h * HEAD, (h + 1) * HEAD)
        memory = got_ref[:, h * 16 : (h + 1) * 16, :].reshape(HEAD, HEAD)
        back = got_ref[:, 32 + h * 16 : 48 + h * 16, :].reshape(HEAD, HEAD)
        starts, ends, backs = [], [], [None] * PARTS
        keeps = []
        for c in range(PARTS):
            _, _, first, last = seg[c]
            end = decay_ref[(c + 1) * CHUNK - 1 : (c + 1) * CHUNK, on]
            keeps.append(jnp.exp(end) * as_number(first == last))
            if c > 0:
                memory = memory * as_number(first == seg[c - 1][3])
            starts.append(memory)
            memory = mem_ref[h, c] + keeps[c] * memory
            ends.append(memory)
        for c in reversed(range(PARTS)):
            backs[c] = back
            if c > 0:
                back = as_number(seg[c][2] == seg[c - 1][3]) * (pull_ref[h, c] + keeps[c] * back)
        for c in range(PARTS):
            at = slice(c * CHUNK, (c + 1) * CHUNK)
            _, column, first, last = seg[c]
            lead, tail = as_number(column == first), as_number(column == last)
            q, k, v, d = q_ref[at, on], k_ref[at, on], v_ref[at, on], d_ref[at, on]
            q32, k32 = q.astype(F32), k.astype(F32)
            decay = decay_ref[at, on]
            end = decay[CHUNK - 1 :, :]
            grow = jnp.exp(decay)
            shrink = jnp.exp(-decay)
            rest = jnp.exp(end - decay) * tail
            qd = split2(q32 * grow)
            kd = split2(k32 * shrink)
            kt = split2(k32 * rest)
            start, behind = split2(starts[c]), split2(backs[c])
            scores = split2(jnp.where(masks[c], dot_both(qd, kd, NT), 0.0))
            pulls = split2(jnp.where(masks[c], dot(d, v, NT), 0.0))
            out = dot_right(scores, v, NN) + lead * dot_both(qd, start, NT)
            out_ref[at, on] = (out * SCALE).astype(BF16)
            dq = (dot_both(pulls, kd, NN) + lead * dot_left(d, start, NN)) * (grow * SCALE)
            dk = dot_both(pulls, qd, TN) * (shrink * SCALE) + rest * dot_left(v, behind, NN)
            dv = dot_right(scores, d, TN) * SCALE + dot_both(kt, behind, NT)
            dq_ref[at, on] = dq.astype(BF16)
            dk_ref[at, on] = dk.astype(BF16)
            dv_ref[at, on] = dv.astype(BF16)
            through = jnp.sum(ends[c] * backs[c], axis=0, keepdims=True)
            grad_gate = dot_left(later[c], split3(q32 * dq - k32 * dk), NN) + tail * through
            grad_pre = grad_gate * slope_ref[at, on]
            grad_b[h] = jnp.sum(grad_pre, axis=0, keepdims=True) + (0.0 if c == 0 else grad_b[h])
            grad_pre_parts[c][h] = split2(grad_pre)
    w = w_ref[...]
    lat_parts = []
    for c in range(PARTS):
        pre = tuple(
            jnp.concatenate([grad_pre_parts[c][h][i] for h in range(heads)], axis=1) for i in range(2)
        )
        lat_parts.append(dot(w, pre[0], NT) + dot(w, pre[1], NT))
        lat = lat_ref[:, c * CHUNK : (c + 1) * CHUNK]
        for h in range(heads):
            add = dot_left(lat, grad_pre_parts[c][h], NN)
            grad_w[h] = add if c == 0 else grad_w[h] + add
    zeros = jnp.zeros((7, HEAD), F32)
    lat_send = jnp.concatenate(lat_parts, axis=0)
    w_send = jnp.concatenate(
        [x for h in range(heads) for x in (grad_w[h], grad_b[h], zeros)], axis=0
    )
    for j in range(RING):
        lat_send_ref[j] = lat_send
        w_send_ref[j] = w_send


def resend_kernel(got_ref, send_ref):
    total = got_ref[0]
    for j in range(1, RING):
        total = total + got_ref[j]
    for j in range(RING):
        send_ref[j] = total


def finish_kernel(lat_got_ref, w_got_ref, lat_ref, w_ref, b_ref):
    total = lat_got_ref[0]
    for j in range(1, RING):
        total = total + lat_got_ref[j]
    for c in range(PARTS):
        lat_ref[:, c * CHUNK : (c + 1) * CHUNK] = total[c * RANK : (c + 1) * RANK, :]
    total = w_got_ref[0]
    for j in range(1, RING):
        total = total + w_got_ref[j]
    for h in range(2):
        on = slice(h * HEAD, (h + 1) * HEAD)
        w_ref[:, on] = total[h * 24 : h * 24 + RANK, :]
        b_ref[:, on] = total[h * 24 + RANK : h * 24 + RANK + 1, :]


def call(kernel, outs, *operands):
    whole = pl.BlockSpec(memory_space=pltpu.VMEM)
    return pl.pallas_call(
        kernel,
        out_shape=outs,
        in_specs=[whole] * len(operands),
        out_specs=jax.tree.map(lambda _: whole, outs),
        compiler_params=pltpu.CompilerParams(vmem_limit_bytes=40 * 2**20),
    )(*operands)


def shape(dims, kind=F32):
    return jax.ShapeDtypeStruct(dims, kind)


def exchange(x, axis):
    return lax.all_to_all(x, axis, 0, 0)


def passed(value, axis, steps):
    count = lax.axis_size(axis)
    pairs = [(s, s + steps) for s in range(count) if 0 <= s + steps < count]
    return lax.ppermute(value, axis, pairs)


def body(query, key_in, value, latent, w_b, gate_bias, doc_ids, d_out):
    tokens, width = query.shape
    heads = width // HEAD
    lat = latent.T
    bias = gate_bias.reshape(1, width)
    docs = doc_ids.astype(F32).reshape(PARTS, CHUNK)
    wide = shape((tokens, width))
    states = shape((heads, PARTS, HEAD, HEAD))
    send, decay, slope, mem, pull = call(
        state_kernel, (shape((RING, 72, HEAD)), wide, wide, states, states),
        lat, w_b, bias, docs, query, key_in, value, d_out,
    )
    got = exchange(send, "y")
    ahead, behind = call(total_kernel, (shape((40, HEAD)), shape((40, HEAD))), got)
    ahead, behind = passed(ahead, "z", 1), passed(behind, "z", -1)
    back = call(spread_kernel, shape((RING, 64, HEAD)), got, ahead, behind)
    carried = exchange(back, "y")
    half = shape((tokens, width), BF16)
    out, grad_q, grad_k, grad_v, lat_send, w_send = call(
        main_kernel,
        (half, half, half, half, shape((RING, PARTS * RANK, HEAD)), shape((RING, 48, HEAD))),
        lat, w_b, docs, query, key_in, value, d_out, decay, slope, mem, pull, carried,
    )
    w_got = exchange(w_send, "y")
    w_send = call(resend_kernel, shape((RING, 48, HEAD)), w_got)
    w_got = exchange(w_send, "z")
    lat_got = exchange(lat_send, DP)
    grad_lat, grad_w, grad_b = call(
        finish_kernel, (shape((RANK, tokens)), shape((RANK, width)), shape((1, width))), lat_got, w_got
    )
    return out, grad_q, grad_k, grad_v, grad_lat.T, grad_w, grad_b.reshape(width)


def solution(mesh):
    grid = Mesh(mesh.devices.reshape(4, 2, RING, RING), ("x", "core", "z", "y"))
    rows = P(CTX, DP)
    in_specs = (rows, rows, rows, P(CTX, None), P(None, DP), P(DP), P(CTX), rows)
    out_specs = (rows, rows, rows, rows, P(CTX, None), P(None, DP), P(DP))
    return jax.shard_map(body, mesh=grid, in_specs=in_specs, out_specs=out_specs, check_vma=False)
```

time: 830 us -> 100 us (0.12)
  blocking collectives: 422 us -> 63.9 us
  other arithmetic: 134 us -> 0.68 us
  local copies, waits for them, and re-layouts: 91.7 us -> 5.91 us
  waiting for transfers between devices: 75.9 us -> 10.2 us
  matrix products: 65.4 us -> 0 us
  between operations: 15.8 us -> 0.7 us
  loops' own time: 13.7 us -> 0 us
    psum x2 -> x0, blocking collectives: 367 us -> none  [the longest x1 345 us: body(): grad_weight, grad_bias = lax.psum((grad_weight, grad_bias), 'ctx')]
    all_gather x2 -> x0, waiting for transfers between devices: 75.9 us -> none  [prefix(): gathered = jax.tree.map(lambda a: lax.all_gather(a, axis), part)]
    dot_general x101 -> x0, matrix products: 65.4 us -> none  [the longest x24 23.3 us: group_pass(): jnp.einsum('hij,jhv->ihv', scores, values_portion, precision=precise_mode)]
    add x63 -> x0, other arithmetic: 64.7 us -> none  [affine_combine(): later_pair[1] + later_pair[0][..., None] * earlier[1]]
    all_to_all x0 -> x4, blocking collectives: none -> 63.9 us  [exchange(): return lax.all_to_all(x, axis, 0, 0)]
    all_gather x1 -> x0, blocking collectives: 55.4 us -> none  [prefix(): gathered = jax.tree.map(lambda a: lax.all_gather(a, axis), part)]
    dynamic_slice x56 -> x0, local copies, waits for them, and re-layouts: 36.4 us -> none  [device_pass(): lax.scan(group_pass, (memory_in, prev_id), pieces + (segment.reshape(-1,...]
    dynamic_update_slice x32 -> x0, other arithmetic: 30.9 us -> none  [device_pass(): lax.scan(group_pass, (memory_in, prev_id), pieces + (segment.reshape(-1,...]
  transfers between devices with their start and end apart: 3 -> 3, of which waited for: 2 -> 3; matrix products, arithmetic and copies ran while one was open for 9% -> 0% of each run, Pallas kernels for 0% -> 0%
where the time goes in v1:
time: 100 us; the launch traced here: 99 us
  blocking collectives  63.9 us (64%)
  starting transfers between devices  10.4 us (10%)
  waiting for transfers between devices  10.2 us (10%)
  Pallas kernels  7.25 us (7%)
  local copies, waits for them, and re-layouts  5.91 us (6%)
    all_to_all x4, blocking collectives, exchange(): return lax.all_to_all(x, axis, 0, 0)  63.9 us
    pallas_call x6, Pallas kernels, call(): pl.pallas_call(kernel, out_shape=outs, in_specs=[whole] * len(operands),...  7.25 us
    unnamed x22, local copies, waits for them, and re-layouts  5.91 us
    ppermute x2, starting transfers between devices, passed(): return lax.ppermute(value, axis, pairs)  5.57 us
    all_to_all x1, waiting for transfers between devices, exchange(): return lax.all_to_all(x, axis, 0, 0)  5.45 us
    all_to_all x1, starting transfers between devices, exchange(): return lax.all_to_all(x, axis, 0, 0)  4.78 us
    ppermute x2, waiting for transfers between devices, passed(): return lax.ppermute(value, axis, pairs)  4.73 us
  transfers between devices with their start and end apart: 3, of which 3 were waited for; matrix products, arithmetic and copies ran while one was open for 0% of the time, Pallas kernels for 0%

profile of v1, /device:TPU:6, one launch (start us, length us, event | category | flops | bytes accessed | tf_op | source)
XLA Modules:
  0.0 99.0 jit_solution(11197138050152118131)
XLA Ops:
  0.6 0.7 convert_bitcast_fusion.doc_ref
  1.3 0.7 copy-done.10
  2.0 0.9 copy-done
  2.9 0.9 copy-done.2
  3.9 0.9 copy-done.4
  4.8 0.9 copy-done.6
  5.8 0.7 copy-done.8
  6.5 0.7 copy-done.9
  7.2 1.6 %shard_map.135 = (f32[8,72,128]{2,1,0:T(8,128)S(1)}, f32[512,256]{1,0:T(8,128)S(1)}, f32[512,256]{1,0:T(8,128)S(1)}, f32[2,4,128,128]{3,2,1,0:T(8,128)S(1)}, f32[2,4,128,128]{3,2,1,0:T(8,128)S(1)}) custom-call(bf16[16,512]{1,0:T(8,128)(2,1)S(1)} %bitcast.6, bf16[16,256]{1,0:T(8,128)(2,1)S(1)} %copy-done.9, f32[1,256]{1,0:T(1,128)S(1)} %bitcast.8, ...), custom_call_target="tpu_custom_call" | custom-call | tf_op jit(solution)/shard_map/pallas_call | solution.py:284
  8.8 19.5 %all_to_all.25.got_ref = f32[8,72,128]{2,1,0:T(8,128)S(1)} all-to-all(f32[8,72,128]{2,1,0:T(8,128)S(1)} %get-tuple-element.27), channel_id=1, replica_groups=mesh['x'=4,'core'=2,'z'=8,'y'=8] {'y'}, dimensions={0} | all-to-all | bytes 589824 | tf_op jit(solution)/shard_map/all_to_all | solution.py:298
  28.3 4.3 %collective-permute-start = (f32[40,128]{1,0:T(8,128)S(1)}, f32[40,128]{1,0:T(8,128)S(1)}, u32[]{:S(2)}, u32[]{:S(2)}) collective-permute-start(f32[40,128]{1,0:T(8,128)S(1)} %get-tuple-element.28), channel_id=1, source_target_pairs={{0,8},{8,16},{16,24},{24,32},{32,40},{40,48},{48,56},{1,9},{9,17},... | collective-permute-start | bytes 61448 | tf_op jit(solution)/shard_map/ppermute | solution.py:304
  32.6 1.3 %collective-permute-start.1 = (f32[40,128]{1,0:T(8,128)S(1)}, f32[40,128]{1,0:T(8,128)S(1)}, u32[]{:S(2)}, u32[]{:S(2)}) collective-permute-start(f32[40,128]{1,0:T(8,128)S(1)} %get-tuple-element.29), channel_id=1, source_target_pairs={{8,0},{16,8},{24,16},{32,24},{40,32},{48,40},{56,48},{9,1},{17,9},... | collective-permute-start | bytes 61448 | tf_op jit(solution)/shard_map/ppermute | solution.py:304
  33.9 0.2 collective-permute-done.ahead_ref
  34.0 4.6 %collective-permute-done.1.behind_ref = f32[40,128]{1,0:T(8,128)S(1)} collective-permute-done((f32[40,128]{1,0:T(8,128)S(1)}, f32[40,128]{1,0:T(8,128)S(1)}, u32[]{:S(2)}, u32[]{:S(2)}) %collective-permute-start.1) | collective-permute-done | bytes 20512 | tf_op jit(solution)/shard_map/ppermute | solution.py:304
  38.7 0.0 copy-start.1
  38.7 0.0 copy-start.3
  38.7 13.0 %all_to_all.26.got_ref = f32[8,64,128]{2,1,0:T(8,128)S(1)} all-to-all(f32[8,64,128]{2,1,0:T(8,128)S(1)} %shard_map.137), channel_id=1, replica_groups=mesh['x'=4,'core'=2,'z'=8,'y'=8] {'y'}, dimensions={0} | all-to-all | bytes 524288 | tf_op jit(solution)/shard_map/all_to_all | solution.py:298
  51.7 0.0 copy-done.1
  51.7 5.0 %shard_map.138 = (bf16[512,256]{1,0:T(8,128)(2,1)}, bf16[512,256]{1,0:T(8,128)(2,1)}, bf16[512,256]{1,0:T(8,128)(2,1)}, bf16[512,256]{1,0:T(8,128)(2,1)}, f32[8,...) custom-call(bf16[16,512]{1,0:T(8,128)(2,1)S(1)} %bitcast.7, bf16[16,256]{1,0:T(8,128)(2,1)S(1)} %copy-done.9, ...), custom_call_target="tpu_custom_call" | custom-call | tf_op jit(solution)/shard_map/pallas_call | solution.py:284
  56.7 12.2 %all_to_all.27.got_ref = f32[8,48,128]{2,1,0:T(8,128)S(1)} all-to-all(f32[8,48,128]{2,1,0:T(8,128)S(1)} %get-tuple-element.35), channel_id=1, replica_groups=mesh['x'=4,'core'=2,'z'=8,'y'=8] {'y'}, dimensions={0} | all-to-all | bytes 393216 | tf_op jit(solution)/shard_map/all_to_all | solution.py:298
  68.8 4.8 %all-to-all-start.2 = ((f32[8,64,128]{2,1,0:T(8,128)}), f32[8,64,128]{2,1,0:T(8,128)S(1)}, u32[]{:S(2)}, u32[]{:S(2)}) async-start(f32[8,64,128]{2,1,0:T(8,128)} %get-tuple-element.34), calls=%async_computation.2 | async-start | bytes 524288 | tf_op jit(solution)/shard_map/all_to_all | solution.py:298
  73.6 5.4 %all-to-all-done.2.lat_got_ref = f32[8,64,128]{2,1,0:T(8,128)S(1)} async-done(((f32[8,64,128]{2,1,0:T(8,128)}), f32[8,64,128]{2,1,0:T(8,128)S(1)}, u32[]{:S(2)}, u32[]{:S(2)}) %all-to-all-start.2) | async-done | bytes 262176 | tf_op jit(solution)/shard_map/all_to_all | solution.py:298
  79.1 19.2 %all_to_all.28.w_got_ref = f32[8,48,128]{2,1,0:T(8,128)S(1)} all-to-all(f32[8,48,128]{2,1,0:T(8,128)S(1)} %shard_map.139), channel_id=1, replica_groups=mesh['x'=4,'core'=2,'z'=8,'y'=8] {'z'}, dimensions={0} | all-to-all | bytes 393216 | tf_op jit(solution)/shard_map/all_to_all | solution.py:298
  98.3 0.6 shard_map.140
  (15 shorter events, 0.1 us)
Async XLA Ops:
  1.3 0.7 copy-start.10
  2.0 0.9 copy-start
  2.9 0.9 copy-start.2
  3.9 0.9 copy-start.4
  4.8 0.9 copy-start.6
  5.8 0.7 copy-start.8
  6.5 0.7 copy-start.9
  28.3 5.8 %collective-permute-start = (f32[40,128]{1,0:T(8,128)S(1)}, f32[40,128]{1,0:T(8,128)S(1)}, u32[]{:S(2)}, u32[]{:S(2)}) collective-permute-start(f32[40,128]{1,0:T(8,128)S(1)} %get-tuple-element.28), channel_id=1, source_target_pairs={{0,8},{8,16},{16,24},{24,32},{32,40},{40,48},{48,56},{1,9},{9,17},... | collective-permute-start | bytes 61448 | tf_op jit(solution)/shard_map/ppermute | solution.py:304
  32.6 6.0 %collective-permute-start.1 = (f32[40,128]{1,0:T(8,128)S(1)}, f32[40,128]{1,0:T(8,128)S(1)}, u32[]{:S(2)}, u32[]{:S(2)}) collective-permute-start(f32[40,128]{1,0:T(8,128)S(1)} %get-tuple-element.29), channel_id=1, source_target_pairs={{8,0},{16,8},{24,16},{32,24},{40,32},{48,40},{56,48},{9,1},{17,9},... | collective-permute-start | bytes 61448 | tf_op jit(solution)/shard_map/ppermute | solution.py:304
  38.6 13.1 %copy-start.5 = (bf16[512,256]{1,0:T(8,128)(2,1)S(1)}, bf16[512,256]{1,0:T(8,128)(2,1)}, u32[]{:S(2)}) copy-start(bf16[512,256]{1,0:T(8,128)(2,1)} %v_ref.3) | copy-start | bytes 786436
  38.6 13.1 %copy-start.7 = (bf16[512,256]{1,0:T(8,128)(2,1)S(1)}, bf16[512,256]{1,0:T(8,128)(2,1)}, u32[]{:S(2)}) copy-start(bf16[512,256]{1,0:T(8,128)(2,1)} %d_ref.3) | copy-start | bytes 786436
  38.7 13.1 %copy-start.1 = (bf16[512,256]{1,0:T(8,128)(2,1)S(1)}, bf16[512,256]{1,0:T(8,128)(2,1)}, u32[]{:S(2)}) copy-start(bf16[512,256]{1,0:T(8,128)(2,1)} %q_ref.3) | copy-start | bytes 786436
  38.7 13.0 %copy-start.3 = (bf16[512,256]{1,0:T(8,128)(2,1)S(1)}, bf16[512,256]{1,0:T(8,128)(2,1)}, u32[]{:S(2)}) copy-start(bf16[512,256]{1,0:T(8,128)(2,1)} %k_ref.3) | copy-start | bytes 786436
  68.8 10.3 %all-to-all-start.2 = ((f32[8,64,128]{2,1,0:T(8,128)}), f32[8,64,128]{2,1,0:T(8,128)S(1)}, u32[]{:S(2)}, u32[]{:S(2)}) async-start(f32[8,64,128]{2,1,0:T(8,128)} %get-tuple-element.34), calls=%async_computation.2 | async-start | bytes 524288 | tf_op jit(solution)/shard_map/all_to_all | solution.py:298

commit v2 on v1

v2 whole, which is shorter than its diff:
```python
import jax
import jax.numpy as jnp
from jax import lax
from jax.experimental import pallas as pl
from jax.experimental.pallas import tpu as pltpu
from jax.sharding import Mesh
from jax.sharding import PartitionSpec as P

HEAD = 128
RANK = 16
SPAN = 512
CHUNK = 128
PARTS = SPAN // CHUNK
SCALE = HEAD ** (-0.5)
RING = 8
HELD = 16
INNER_HELD = 16
INNER_FLOPS = 4 * 10**10
CTX = ("z", "y")
DP = ("x", "core")

F32 = jnp.float32
BF16 = jnp.bfloat16
NN = (((1,), (0,)), ((), ()))
NT = (((1,), (1,)), ((), ()))
TN = (((0,), (0,)), ((), ()))


def split2(x):
    high = x.astype(BF16)
    return high, (x - high.astype(F32)).astype(BF16)


def split3(x):
    high = x.astype(BF16)
    rest = x - high.astype(F32)
    middle = rest.astype(BF16)
    return high, middle, (rest - middle.astype(F32)).astype(BF16)


def dot(a, b, dims):
    return lax.dot_general(a, b, dims, preferred_element_type=F32)


def dot_left(a, parts, dims):
    (ca,), (cb,) = dims[0]
    return dot(jnp.concatenate([a] * len(parts), axis=ca), jnp.concatenate(parts, axis=cb), dims)


def dot_right(parts, b, dims):
    (ca,), (cb,) = dims[0]
    return dot(jnp.concatenate(parts, axis=ca), jnp.concatenate([b] * len(parts), axis=cb), dims)


def dot_both(a, b, dims):
    (ca,), (cb,) = dims[0]
    left = jnp.concatenate([a[0], a[1], a[0]], axis=ca)
    right = jnp.concatenate([b[0], b[0], b[1]], axis=cb)
    return dot(left, right, dims)


def places():
    rows = lax.broadcasted_iota(jnp.int32, (CHUNK, CHUNK), 0)
    columns = lax.broadcasted_iota(jnp.int32, (CHUNK, CHUNK), 1)
    return rows, columns


def segments(doc_ref, c):
    rows, columns = places()
    row = doc_ref[c : c + 1, :].astype(F32)
    column = jnp.sum(jnp.where(rows == columns, row, 0.0), axis=1, keepdims=True)
    return row, column, row[:, :1], row[:, CHUNK - 1 :]


def chunk(c):
    return slice(c * CHUNK, (c + 1) * CHUNK)


def head(h):
    return slice(h * HEAD, (h + 1) * HEAD)


def as_number(flag):
    return flag.astype(F32)


def gates(lat_ref, w_ref, bias_ref):
    gate_pre = dot(lat_ref[...], w_ref[...], TN) + bias_ref[...]
    small = jnp.exp(-jnp.abs(gate_pre))
    series = small * (1.0 - small * (0.5 - small * (1.0 / 3.0 - small * (0.25 - small * 0.2))))
    log_one = jnp.where(small < 0.02, series, jnp.log(1.0 + small))
    log_gate = -(jnp.maximum(-gate_pre, 0.0) + log_one) / 16.0
    sigmoid = jnp.where(gate_pre >= 0.0, small, 1.0) / (1.0 + small)
    free = jnp.where(log_gate > -0.5, 1.0, jnp.where(log_gate == -0.5, 0.5, 0.0))
    return jnp.maximum(log_gate, -0.5), free * sigmoid * (1.0 / 16.0)


def decays(log_gate):
    rows, columns = places()
    lower3 = jnp.concatenate([(rows >= columns).astype(BF16)] * 3, axis=1)
    return [
        dot(lower3, jnp.concatenate(split3(log_gate[chunk(c), :]), axis=0), NN) for c in range(PARTS)
    ]


def state_kernel(ins, outs, need, emit):
    lat_ref, w_ref, bias_ref, doc_ref, k_ref, v_ref, q_ref, d_ref = ins
    send_ref, gate_ref, state_ref = outs
    heads = q_ref.shape[1] // HEAD
    need(0, 1, 2, 3)
    log_gate, gate_ref[1] = gates(lat_ref, w_ref, bias_ref)
    decay = decays(log_gate)
    for c in range(PARTS):
        gate_ref[0, chunk(c), :] = decay[c]
    emit(1, slice(None))
    seg = [segments(doc_ref, c) for c in range(PARTS)]
    first, last = seg[0][2], seg[-1][3]
    ends = [decay[c][CHUNK - 1 :, :] for c in range(PARTS)]
    grow = [jnp.exp(decay[c]) * (as_number(seg[c][1] == seg[c][2]) * SCALE) for c in range(PARTS)]
    rest = [jnp.exp(ends[c] - decay[c]) * as_number(seg[c][1] == seg[c][3]) for c in range(PARTS)]
    keep = [jnp.exp(ends[c]) * as_number(seg[c][2] == seg[c][3]) for c in range(PARTS)]
    link = [as_number(seg[c][2] == seg[c - 1][3]) for c in range(1, PARTS)]
    whole = jnp.exp(sum(ends)) * as_number(first == last)
    need(4, 5, 6, 7)
    each = HEAD // RING
    for h in range(heads):
        on = head(h)
        for c in range(PARTS):
            at = chunk(c)
            added = dot_left(v_ref[at, on], split2(k_ref[at, on].astype(F32) * rest[c][:, on]), TN)
            state_ref[0, h, c] = added
            state_ref[1, h, c] = dot_left(
                d_ref[at, on], split2(q_ref[at, on].astype(F32) * grow[c][:, on]), TN
            )
            memory = added if c == 0 else added + keep[c][:, on] * link[c - 1] * memory
        emit(2, (slice(None), h))
        back = state_ref[1, h, PARTS - 1]
        for c in reversed(range(PARTS - 1)):
            back = state_ref[1, h, c] + keep[c][:, on] * link[c] * back
        for j in range(RING):
            send_ref[j, h * each : (h + 1) * each, :] = memory[j * each : (j + 1) * each, :]
            start = heads * each + h * each
            send_ref[j, start : start + each, :] = back[j * each : (j + 1) * each, :]
    small_rows = jnp.concatenate(
        [whole[:, head(h)] for h in range(heads)]
        + [jnp.broadcast_to(first + 1.0, (1, HEAD)), jnp.broadcast_to(last + 1.0, (1, HEAD))]
        + [jnp.zeros((4, HEAD), F32)],
        axis=0,
    )
    for j in range(RING):
        send_ref[j, 64:, :] = small_rows
    emit(0, slice(None))


def taken(got_ref, j):
    factor = jnp.concatenate(
        [jnp.broadcast_to(got_ref[j, 64 + h : 65 + h, :], (16, HEAD)) for h in range(2)], axis=0
    )
    return got_ref[j, 0:32, :], got_ref[j, 32:64, :], factor, got_ref[j, 66:67, :], got_ref[j, 67:68, :]


def total_kernel(got_ref, sum_ref, ahead_ref, behind_ref):
    got = [taken(got_ref, j) for j in range(RING)]
    memory = got[0][0]
    for j in range(1, RING):
        memory = got[j][0] + got[j][2] * as_number(got[j][3] == got[j - 1][4]) * memory
    back = got[-1][1]
    for j in reversed(range(RING - 1)):
        back = got[j][1] + got[j][2] * as_number(got[j][4] == got[j + 1][3]) * back
    zeros = jnp.zeros((7, HEAD), F32)
    ahead_ref[...] = jnp.concatenate([memory, got[-1][4], zeros], axis=0)
    behind_ref[...] = jnp.concatenate([back, got[0][3], zeros], axis=0)


def spread_kernel(got_ref, ahead_ref, behind_ref, send_ref):
    got = [taken(got_ref, j) for j in range(RING)]
    memory = as_number(got[0][3] == ahead_ref[32:33, :]) * ahead_ref[0:32, :]
    for j in range(RING):
        send_ref[j, 0:32, :] = memory
        if j < RING - 1:
            memory = as_number(got[j][4] == got[j + 1][3]) * (got[j][0] + got[j][2] * memory)
    back = as_number(got[-1][4] == behind_ref[32:33, :]) * behind_ref[0:32, :]
    for j in reversed(range(RING)):
        send_ref[j, 32:64, :] = back
        if j > 0:
            back = as_number(got[j - 1][4] == got[j][3]) * (got[j][1] + got[j][2] * back)


def backward_sums(change, mask):
    return dot_left(mask, split3(change), NN)


def gate_sums(grad_pre, lat_ref, w_ref):
    heads = len(grad_pre[0])
    parts = [[split2(x) for x in row] for row in grad_pre]
    w = w_ref[...]
    lat_parts = []
    for c in range(PARTS):
        pre = [jnp.concatenate([parts[c][h][i] for h in range(heads)], axis=1) for i in range(2)]
        lat_parts.append(dot(w, pre[0], NT) + dot(w, pre[1], NT))
    lat = jnp.concatenate([lat_ref[...]] * 2, axis=1)
    grad_w, grad_b = [], []
    for h in range(heads):
        column = [parts[c][h][i] for i in range(2) for c in range(PARTS)]
        grad_w.append(dot(lat, jnp.concatenate(column, axis=0), NN))
        total = sum(grad_pre[c][h] for c in range(PARTS))
        grad_b.append(jnp.sum(total, axis=0, keepdims=True))
    zeros = jnp.zeros((6, HEAD), F32)
    return jnp.concatenate(lat_parts, axis=0), jnp.concatenate(grad_w + grad_b + [zeros], axis=0)


def inner_kernel(ins, outs, need, emit):
    lat_ref, w_ref, bias_ref, doc_ref, k_ref, v_ref, q_ref, d_ref = ins
    term_ref, sum_ref = outs
    heads = q_ref.shape[1] // HEAD
    rows, columns = places()
    log_gate, slope = gates(lat_ref, w_ref, bias_ref)
    decays_here = decays(log_gate)
    grad_pre = [[None] * heads for _ in range(PARTS)]
    for c in range(PARTS):
        row, column, _, _ = segments(doc_ref, c)
        same = column == row
        mask = (rows >= columns) & same
        later = ((columns >= rows) & same).astype(BF16)
        at = chunk(c)
        for h in range(heads):
            on = head(h)
            v, d = v_ref[at, on], d_ref[at, on]
            q32, k32 = q_ref[at, on].astype(F32), k_ref[at, on].astype(F32)
            decay = decays_here[c][:, on]
            grow, shrink = jnp.exp(decay), jnp.exp(-decay)
            qd, kd = split2(q32 * grow), split2(k32 * shrink)
            scores = split2(jnp.where(mask, dot_both(qd, kd, NT), 0.0))
            pulls = split2(jnp.where(mask, dot(d, v, NT), 0.0))
            term_ref[0, at, on] = dot_right(scores, v, NN) * SCALE
            term_ref[3, at, on] = dot_right(scores, d, TN) * SCALE
            dq = dot_both(pulls, kd, NN) * (grow * SCALE)
            dk = dot_both(pulls, qd, TN) * (shrink * SCALE)
            term_ref[1, at, on] = dq
            term_ref[2, at, on] = dk
            grad_pre[c][h] = backward_sums(q32 * dq - k32 * dk, later) * slope[at, on]
        emit(0, (slice(None), at))
    sum_ref[: PARTS * RANK, :], sum_ref[PARTS * RANK :, :] = gate_sums(grad_pre, lat_ref, w_ref)


def carry(h, seg, gate_ref, state_ref, got_ref):
    memory = got_ref[:, h * 16 : (h + 1) * 16, :].reshape(HEAD, HEAD)
    back = got_ref[:, 32 + h * 16 : 48 + h * 16, :].reshape(HEAD, HEAD)
    starts, ends, backs, keeps = [], [], [None] * PARTS, []
    for c in range(PARTS):
        _, _, first, last = seg[c]
        end = gate_ref[0, (c + 1) * CHUNK - 1 : (c + 1) * CHUNK, head(h)]
        keeps.append(jnp.exp(end) * as_number(first == last))
        if c > 0:
            memory = memory * as_number(first == seg[c - 1][3])
        starts.append(memory)
        memory = state_ref[0, h, c] + keeps[c] * memory
        ends.append(memory)
    for c in reversed(range(PARTS)):
        backs[c] = back
        if c > 0:
            back = as_number(seg[c][2] == seg[c - 1][3]) * (state_ref[1, h, c] + keeps[c] * back)
    return starts, ends, backs


def crossing(seg, c, h, q_ref, k_ref, v_ref, d_ref, gate_ref, start, behind):
    at, on = chunk(c), head(h)
    _, column, first, last = seg[c]
    decay = gate_ref[0, at, on]
    grow = jnp.exp(decay) * as_number(column == first)
    rest = jnp.exp(decay[CHUNK - 1 :, :] - decay) * as_number(column == last)
    dq = dot_left(d_ref[at, on], start, NN) * (grow * SCALE)
    dk = dot_left(v_ref[at, on], behind, NN) * rest
    return q_ref[at, on].astype(F32), k_ref[at, on].astype(F32), grow, rest, dq, dk


def grad_kernel(ins, outs, need, emit):
    got_ref, doc_ref, gate_ref, state_ref, v_ref, d_ref, q_ref, k_ref, lat_ref, w_ref, sum_ref = ins
    lat_send_ref, w_send_ref = outs
    heads = q_ref.shape[1] // HEAD
    rows, columns = places()
    seg = [segments(doc_ref, c) for c in range(PARTS)]
    later = [((columns >= rows) & (seg[c][1] == seg[c][0])).astype(BF16) for c in range(PARTS)]
    carried = [carry(h, seg, gate_ref, state_ref, got_ref) for h in range(heads)]
    grad_pre = [[None] * heads for _ in range(PARTS)]
    for h in range(heads):
        starts, ends, backs = carried[h]
        for c in range(PARTS):
            q32, k32, _, _, dq, dk = crossing(
                seg, c, h, q_ref, k_ref, v_ref, d_ref, gate_ref, split2(starts[c]), split2(backs[c])
            )
            through = jnp.sum(ends[c] * backs[c], axis=0, keepdims=True)
            tail = as_number(seg[c][1] == seg[c][3])
            grad_gate = backward_sums(q32 * dq - k32 * dk, later[c]) + tail * through
            grad_pre[c][h] = grad_gate * gate_ref[1, chunk(c), head(h)]
    lat_sum, w_sum = gate_sums(grad_pre, lat_ref, w_ref)
    lat_send_ref[...] = lat_sum + sum_ref[: PARTS * RANK, :]
    w_sum = w_sum + sum_ref[PARTS * RANK :, :]
    for j in range(RING):
        w_send_ref[j] = w_sum


def outer_kernel(ins, outs, need, emit):
    got_ref, doc_ref, gate_ref, state_ref, v_ref, d_ref, q_ref, k_ref, term_ref = ins
    out_ref, dq_ref, dk_ref, dv_ref = outs
    heads = q_ref.shape[1] // HEAD
    need(0, 1, 2, 3)
    seg = [segments(doc_ref, c) for c in range(PARTS)]
    carried = [carry(h, seg, gate_ref, state_ref, got_ref) for h in range(heads)]
    need(4, 5, 6, 7, 8)
    for c in range(PARTS):
        at = chunk(c)
        for h in range(heads):
            on = head(h)
            start, behind = split2(carried[h][0][c]), split2(carried[h][2][c])
            q32, k32, grow, rest, dq, dk = crossing(
                seg, c, h, q_ref, k_ref, v_ref, d_ref, gate_ref, start, behind
            )
            out = dot_both(split2(q32 * grow), start, NT) * SCALE
            dv = dot_both(split2(k32 * rest), behind, NT)
            out_ref[at, on] = (term_ref[0, at, on] + out).astype(BF16)
            dq_ref[at, on] = (term_ref[1, at, on] + dq).astype(BF16)
            dk_ref[at, on] = (term_ref[2, at, on] + dk).astype(BF16)
            dv_ref[at, on] = (term_ref[3, at, on] + dv).astype(BF16)
        for i in range(4):
            emit(i, at)


def resend_kernel(got_ref, lat_ref, lat_got_ref, send_ref, lat_send_ref):
    total = got_ref[0]
    for j in range(1, RING):
        total = total + got_ref[j]
    for j in range(RING):
        send_ref[j] = total
    lat_send_ref[...] = lat_ref[...] + lat_got_ref[...]


def finish_kernel(lat_mine_ref, lat_got_ref, w_got_ref, lat_ref, w_ref, b_ref):
    total = lat_mine_ref[...] + lat_got_ref[...]
    for c in range(PARTS):
        lat_ref[:, c * CHUNK : (c + 1) * CHUNK] = total[c * RANK : (c + 1) * RANK, :]
    total = w_got_ref[0]
    for j in range(1, RING):
        total = total + w_got_ref[j]
    for h in range(2):
        on = slice(h * HEAD, (h + 1) * HEAD)
        w_ref[:, on] = total[h * RANK : (h + 1) * RANK, :]
        b_ref[:, on] = total[2 * RANK + h : 2 * RANK + h + 1, :]


def estimate(operands, flops):
    moved = sum(x.size * x.dtype.itemsize for x in operands)
    return pl.CostEstimate(flops=flops, bytes_accessed=moved, transcendentals=0)


def call(kernel, outs, *operands):
    return pl.pallas_call(
        kernel,
        out_shape=outs,
        in_specs=[pl.BlockSpec(memory_space=pltpu.VMEM)] * len(operands),
        out_specs=jax.tree.map(lambda _: pl.BlockSpec(memory_space=pltpu.VMEM), outs),
        cost_estimate=estimate(operands, 10**10),
        compiler_params=pltpu.CompilerParams(vmem_limit_bytes=16 * 2**20),
    )(*operands)


def call_streamed(kernel, outs, *operands, flops, read=True, write=None, limit=60):
    n, m = len(operands), len(outs)
    pieces = 16
    write = tuple(range(m)) if write is None else write

    def run(*refs):
        sources, results, refs = refs[:n], refs[n : n + m], refs[n + m :]
        ins, refs = (refs[:n], refs[n:]) if read else (sources, refs)
        held = list(results)
        for i, buffer in zip(write, refs, strict=False):
            held[i] = buffer
        arrived, sent = refs[-2:]
        copies = [pltpu.make_async_copy(sources[i], ins[i], arrived.at[i]) for i in range(n)] if read else []
        for copy in copies:
            copy.start()
        going = []

        def need(*which):
            for i in which if read else ():
                copies[i].wait()

        def emit(i, at):
            if i in write:
                copy = pltpu.make_async_copy(held[i].at[at], results[i].at[at], sent.at[len(going)])
                copy.start()
                going.append(copy)

        kernel(ins, held, need, emit)
        for copy in going:
            copy.wait()

    spaces = (pltpu.VMEM, pltpu.HBM)
    buffers = [pltpu.VMEM(x.shape, x.dtype) for x in (operands if read else ())]
    buffers += [pltpu.VMEM(outs[i].shape, outs[i].dtype) for i in write]
    return pl.pallas_call(
        run,
        out_shape=outs,
        in_specs=[pl.BlockSpec(memory_space=spaces[read])] * n,
        out_specs=tuple(pl.BlockSpec(memory_space=spaces[i in write]) for i in range(m)),
        scratch_shapes=[*buffers, pltpu.SemaphoreType.DMA((n,)), pltpu.SemaphoreType.DMA((pieces,))],
        cost_estimate=estimate(operands, flops),
        compiler_params=pltpu.CompilerParams(vmem_limit_bytes=limit * 2**20),
    )(*operands)


def shape(dims, kind=F32):
    return jax.ShapeDtypeStruct(dims, kind)


def exchange(x, axis):
    return lax.all_to_all(x, axis, 0, 0)


def passed(value, axis, steps):
    count = lax.axis_size(axis)
    pairs = [(s, s + steps) for s in range(count) if 0 <= s + steps < count]
    return lax.ppermute(value, axis, pairs)


def swapped(value, axis, bit):
    return lax.ppermute(value, axis, [(s, s ^ bit) for s in range(lax.axis_size(axis))])


def body(query, key_in, value, latent, w_b, gate_bias, doc_ids, d_out):
    tokens, width = query.shape
    heads = width // HEAD
    lat = latent.T
    docs = doc_ids.reshape(PARTS, CHUNK)
    half = shape((tokens, width), BF16)
    ring = shape((RING, 40, HEAD))
    lat_shape = shape((PARTS * RANK, HEAD))
    gate_shape, state_shape = shape((2, tokens, width)), shape((2, heads, PARTS, HEAD, HEAD))
    rows = (value, d_out, query, key_in)
    operands = (lat, w_b, gate_bias.reshape(1, width), docs, key_in, value, query, d_out)
    send, gate, state = call_streamed(
        state_kernel, (shape((RING, 72, HEAD)), gate_shape, state_shape),
        *operands, flops=10**9,
    )
    terms, sums = call_streamed(
        inner_kernel, (shape((4, tokens, width)), shape((PARTS * RANK + 40, HEAD))),
        *operands, flops=INNER_FLOPS, read=False, write=(0,), limit=INNER_HELD,
    )
    got = exchange(send, "y")
    ahead, behind = call(total_kernel, (shape((40, HEAD)), shape((40, HEAD))), got, sums)
    ahead, behind = passed(ahead, "z", 1), passed(behind, "z", -1)
    carried = exchange(call(spread_kernel, shape((RING, 64, HEAD)), got, ahead, behind), "y")
    common = (carried, docs, gate, state, *rows)
    lat_send, w_send = call_streamed(
        grad_kernel, (lat_shape, ring), *common, lat, w_b, sums,
        flops=2 * 10**9, read=False, write=(), limit=HELD,
    )
    results = call_streamed(
        outer_kernel, (half, half, half, half), *common, terms, flops=3 * 10**9
    )
    w_got = exchange(w_send, "y")
    lat_send = jnp.sum(lax.all_gather(lat_send, "core"), axis=0)
    w_send, lat_send = call(
        resend_kernel, (ring, lat_shape), w_got, lat_send, swapped(lat_send, "x", 2)
    )
    w_got = exchange(w_send, "z")
    lat_got = swapped(lat_send, "x", 1)
    grad_lat, grad_w, grad_b = call(
        finish_kernel, (shape((RANK, tokens)), shape((RANK, width)), shape((1, width))),
        lat_send, lat_got, w_got,
    )
    return *results, grad_lat.T, grad_w, grad_b.reshape(width)


def solution(mesh):
    grid = Mesh(mesh.devices.reshape(4, 2, RING, RING), ("x", "core", "z", "y"))
    rows = P(CTX, DP)
    in_specs = (rows, rows, rows, P(CTX, None), P(None, DP), P(DP), P(CTX), rows)
    out_specs = (rows, rows, rows, rows, P(CTX, None), P(None, DP), P(DP))
    return jax.shard_map(body, mesh=grid, in_specs=in_specs, out_specs=out_specs, check_vma=False)
```

time: 100 us -> 84.1 us (0.84)
  blocking collectives: 63.9 us -> 14.7 us
  starting transfers between devices: 10.4 us -> 31.6 us
  Pallas kernels: 7.25 us -> 18.4 us
  waiting for transfers between devices: 10.2 us -> 16.4 us
  local copies, waits for them, and re-layouts: 5.91 us -> 1.38 us
    all_to_all x4 -> x1, blocking collectives: 63.9 us -> 12.9 us  [exchange(): return lax.all_to_all(x, axis, 0, 0)]
    all_to_all x1 -> x3, starting transfers between devices: 4.78 us -> 19.9 us  [exchange(): return lax.all_to_all(x, axis, 0, 0)]
    pallas_call x6 -> x8, Pallas kernels: 7.25 us -> 18.4 us  [the longest x4 17 us: call_streamed(): pl.pallas_call(run, out_shape=outs, in_specs=[pl.BlockSpec(memory_space=s...]
    ppermute x0 -> x2, starting transfers between devices: none -> 6.04 us  [swapped(): lax.ppermute(value, axis, [(s, s ^ bit) for s in range(lax.axis_size(axis...]
    unnamed x22 -> x24, local copies, waits for them, and re-layouts: 5.91 us -> 1.38 us
    ppermute x0 -> x2, waiting for transfers between devices: none -> 3.99 us  [swapped(): lax.ppermute(value, axis, [(s, s ^ bit) for s in range(lax.axis_size(axis...]
    all_to_all x1 -> x3, waiting for transfers between devices: 5.45 us -> 7.69 us  [exchange(): return lax.all_to_all(x, axis, 0, 0)]
    all_gather x0 -> x1, blocking collectives: none -> 1.85 us  [body(): lat_send = jnp.sum(lax.all_gather(lat_send, 'core'), axis=0)]
  transfers between devices with their start and end apart: 3 -> 7, of which waited for: 3 -> 5; matrix products, arithmetic and copies ran while one was open for 0% -> 0% of each run, Pallas kernels for 0% -> 12%
where the time goes in v2:
time: 84.1 us; the launch traced here: 83.4 us
  starting transfers between devices  31.6 us (38%)
  Pallas kernels  18.4 us (22%)
  waiting for transfers between devices  16.4 us (20%)
  blocking collectives  14.7 us (17%)
  local copies, waits for them, and re-layouts  1.38 us (2%)
  between operations  0.88 us (1%)
    all_to_all x3, starting transfers between devices, exchange(): return lax.all_to_all(x, axis, 0, 0)  19.9 us
    pallas_call x4, Pallas kernels, call_streamed(): pl.pallas_call(run, out_shape=outs, in_specs=[pl.BlockSpec(memory_space=s...  17 us
    all_to_all x1, blocking collectives, exchange(): return lax.all_to_all(x, axis, 0, 0)  12.9 us
    all_to_all x3, waiting for transfers between devices, exchange(): return lax.all_to_all(x, axis, 0, 0)  7.69 us
    ppermute x2, starting transfers between devices, swapped(): lax.ppermute(value, axis, [(s, s ^ bit) for s in range(lax.axis_size(axis...  6.04 us
    ppermute x2, starting transfers between devices, passed(): return lax.ppermute(value, axis, pairs)  5.71 us
    ppermute x2, waiting for transfers between devices, passed(): return lax.ppermute(value, axis, pairs)  4.73 us
    ppermute x2, waiting for transfers between devices, swapped(): lax.ppermute(value, axis, [(s, s ^ bit) for s in range(lax.axis_size(axis...  3.99 us
  transfers between devices with their start and end apart: 7, of which 5 were waited for; matrix products, arithmetic and copies ran while one was open for 0% of the time, Pallas kernels for 12%

profile of v2, /device:TPU:6, one launch (start us, length us, event | category | flops | bytes accessed | tf_op | source)
XLA Modules:
  0.0 83.4 jit_solution(15473960560431429899)
XLA Ops:
  0.6 0.0 copy-start.2
  0.7 0.0 copy-start.3
  0.7 3.6 %shard_map.135 = (f32[8,72,128]{2,1,0:T(8,128)}, f32[2,512,256]{2,1,0:T(8,128)}, f32[2,2,4,128,128]{4,3,2,1,0:T(8,128)}) custom-call(bf16[16,512]{1,0:T(8,128)(2,1)} %bitcast.6, bf16[16,256]{1,0:T(8,128)(2,1)} %refs_9_.1, f32[1,256]{1,0:T(1,128)} %bitcast.13, s32[4,128]{1,0:T(4,128)} %bitcast.9, bf16[512,256]{1,0:T(8,128)(2,1)} %refs_7_.7, ...), custom_call_target="tpu_custom_call" | custom-call | flops 1000000000 | bytes 1076224 | tf_op jit(solution)/shard_map/pallas_call | solution.py:401
  4.3 7.1 %all-to-all-start = ((f32[8,72,128]{2,1,0:T(8,128)}), f32[8,72,128]{2,1,0:T(8,128)S(1)}, u32[]{:S(2)}, u32[]{:S(2)}) async-start(f32[8,72,128]{2,1,0:T(8,128)} %get-tuple-element.25), calls=%async_computation | async-start | bytes 589824 | tf_op jit(solution)/shard_map/all_to_all | solution.py:417
  11.5 5.8 %shard_map.136 = (f32[4,512,256]{2,1,0:T(8,128)S(1)}, f32[104,128]{1,0:T(8,128)S(1)}) custom-call(bf16[16,512]{1,0:T(8,128)(2,1)S(1)} %bitcast.7, bf16[16,256]{1,0:T(8,128)(2,1)S(1)} %copy-done.6, f32[1,256]{1,0:T(1,128)S(1)} %bitcast.14, s32[4,128]{1,0:T(4,128)S(1)} %bitcast.11, bf16[512,256]{1,0:T(8,128)(2,1)S(1)} %copy-done.1, ...), custom_call_target="tpu_custom_call" | custom-call | flops 40000000000 | bytes 1076224 | tf_op jit(solution)/shard_map/pallas_call | solution.py:401
  17.3 1.3 %copy-done.11 = f32[4,512,256]{2,1,0:T(8,128)} copy-done((f32[4,512,256]{2,1,0:T(8,128)}, f32[4,512,256]{2,1,0:T(8,128)S(1)}, u32[]{:S(2)}) %copy-start.11) | copy-done | bytes 2097176
  18.6 5.4 %all-to-all-done.got_ref = f32[8,72,128]{2,1,0:T(8,128)S(1)} async-done(((f32[8,72,128]{2,1,0:T(8,128)}), f32[8,72,128]{2,1,0:T(8,128)S(1)}, u32[]{:S(2)}, u32[]{:S(2)}) %all-to-all-start) | async-done | bytes 294944 | tf_op jit(solution)/shard_map/all_to_all | solution.py:417
  24.1 4.3 %collective-permute-start = (f32[40,128]{1,0:T(8,128)S(1)}, f32[40,128]{1,0:T(8,128)S(1)}, u32[]{:S(2)}, u32[]{:S(2)}) collective-permute-start(f32[40,128]{1,0:T(8,128)S(1)} %get-tuple-element.27), channel_id=1, source_target_pairs={{0,8},{8,16},{16,24},{24,32},{32,40},{40,48},{48,56},{1,9},{9,17},... | collective-permute-start | bytes 61448 | tf_op jit(solution)/shard_map/ppermute | solution.py:423
  28.4 1.4 %collective-permute-start.1 = (f32[40,128]{1,0:T(8,128)S(1)}, f32[40,128]{1,0:T(8,128)S(1)}, u32[]{:S(2)}, u32[]{:S(2)}) collective-permute-start(f32[40,128]{1,0:T(8,128)S(1)} %get-tuple-element.28), channel_id=1, source_target_pairs={{8,0},{16,8},{24,16},{32,24},{40,32},{48,40},{56,48},{9,1},{17,9},... | collective-permute-start | bytes 61448 | tf_op jit(solution)/shard_map/ppermute | solution.py:423
  29.8 0.0 collective-permute-done.ahead_ref
  29.8 4.7 %collective-permute-done.1.behind_ref = f32[40,128]{1,0:T(8,128)S(1)} collective-permute-done((f32[40,128]{1,0:T(8,128)S(1)}, f32[40,128]{1,0:T(8,128)S(1)}, u32[]{:S(2)}, u32[]{:S(2)}) %collective-permute-start.1) | collective-permute-done | bytes 20512 | tf_op jit(solution)/shard_map/ppermute | solution.py:423
  34.6 12.9 %all_to_all.20.refs_0_ = f32[8,64,128]{2,1,0:T(8,128)S(1)} all-to-all(f32[8,64,128]{2,1,0:T(8,128)S(1)} %shard_map.138), channel_id=1, replica_groups=mesh['x'=4,'core'=2,'z'=8,'y'=8] {'y'}, dimensions={0} | all-to-all | bytes 524288 | tf_op jit(solution)/shard_map/all_to_all | solution.py:417
  47.5 3.1 %shard_map.140 = (f32[64,128]{1,0:T(8,128)S(1)}, f32[8,40,128]{2,1,0:T(8,128)}) custom-call(f32[8,64,128]{2,1,0:T(8,128)S(1)} %all_to_all.20.refs_0_, s32[4,128]{1,0:T(4,128)S(1)} %bitcast.12, f32[2,512,256]{2,1,0:T(8,128)S(1)} %copy-done.9, f32[2,2,4,128,128]{4,3,2,1,0:T(8,128)S(1)} %copy-done.10, bf16[512,256]{1,0:T(8,128)(2,1)S(1)} %copy-done.2, ...), custom_call_target="tpu_custom_call" | custom-call | flops 2000000000 | bytes 3487744 | tf_op jit(solution)/shard_map/pallas_call | solution.py:401
  50.6 3.4 %all-to-all-start.2 = ((f32[8,40,128]{2,1,0:T(8,128)}), f32[8,40,128]{2,1,0:T(8,128)S(1)}, u32[]{:S(2)}, u32[]{:S(2)}) async-start(f32[8,40,128]{2,1,0:T(8,128)} %get-tuple-element.36), calls=%async_computation.2 | async-start | bytes 327680 | tf_op jit(solution)/shard_map/all_to_all | solution.py:417
  54.0 1.9 %all-gather = f32[128,128]{1,0:T(8,128)S(1)} all-gather(f32[64,128]{1,0:T(8,128)S(1)} %get-tuple-element.37), channel_id=2, replica_groups=mesh['x'=4,'core'=2,'z'=8,'y'=8] {'core'}, dimensions={0}, use_global_device_ids=true | all-gather | bytes 98304 | tf_op jit(solution)/shard_map/all_gather | solution.py:462
  55.8 3.3 %collective-permute-start.2 = (f32[64,128]{1,0:T(8,128)S(1)}, f32[64,128]{1,0:T(8,128)S(1)}, u32[]{:S(2)}, u32[]{:S(2)}) collective-permute-start(f32[64,128]{1,0:T(8,128)S(1)} %reduce_sum.9.lat_ref), channel_id=1, source_target_pairs={{0,256},{128,384},{256,0},{384,128},{1,257},{129,385},{257,1},{385... | collective-permute-start | bytes 98312 | tf_op jit(solution)/shard_map/ppermute | solution.py:427
  59.2 4.0 %collective-permute-done.2.lat_got_ref = f32[64,128]{1,0:T(8,128)S(1)} collective-permute-done((f32[64,128]{1,0:T(8,128)S(1)}, f32[64,128]{1,0:T(8,128)S(1)}, u32[]{:S(2)}, u32[]{:S(2)}) %collective-permute-start.2) | collective-permute-done | bytes 32800 | tf_op jit(solution)/shard_map/ppermute | solution.py:427
  63.1 0.2 all-to-all-done.2.got_ref
  63.3 0.7 shard_map.141
  64.0 9.3 %all-to-all-start.3 = ((f32[8,40,128]{2,1,0:T(8,128)}), f32[8,40,128]{2,1,0:T(8,128)S(1)}, u32[]{:S(2)}, u32[]{:S(2)}) async-start(f32[8,40,128]{2,1,0:T(8,128)} %get-tuple-element.39), calls=%async_computation.3 | async-start | bytes 327680 | tf_op jit(solution)/shard_map/all_to_all | solution.py:417
  73.4 2.7 %collective-permute-start.3 = (f32[64,128]{1,0:T(8,128)S(1)}, f32[64,128]{1,0:T(8,128)S(1)}, u32[]{:S(2)}, u32[]{:S(2)}) collective-permute-start(f32[64,128]{1,0:T(8,128)S(1)} %get-tuple-element.38.lat_mine_ref), channel_id=1, source_target_pairs={{0,128},{128,0},{256,384},{384,256},{1,129},{129,1},{257,385},{385... | collective-permute-start | bytes 98312 | tf_op jit(solution)/shard_map/ppermute | solution.py:427
  76.1 4.6 %shard_map.139 = (bf16[512,256]{1,0:T(8,128)(2,1)}, bf16[512,256]{1,0:T(8,128)(2,1)}, bf16[512,256]{1,0:T(8,128)(2,1)}, bf16[512,256]{1,0:T(8,128)(2,1)}) custom-call(f32[8,64,128]{2,1,0:T(8,128)} %copy-done, s32[4,128]{1,0:T(4,128)} %bitcast.10, f32[2,512,256]{2,1,0:T(8,128)} %get-tuple-element.29.refs_2_, ...), custom_call_target="tpu_custom_call" | custom-call | flops 3000000000 | bytes 5507072 | tf_op jit(solution)/shard_map/pallas_call | solution.py:401
  80.7 2.1 %all-to-all-done.3.w_got_ref = f32[8,40,128]{2,1,0:T(8,128)S(1)} async-done(((f32[8,40,128]{2,1,0:T(8,128)}), f32[8,40,128]{2,1,0:T(8,128)S(1)}, u32[]{:S(2)}, u32[]{:S(2)}) %all-to-all-start.3) | async-done | bytes 163872 | tf_op jit(solution)/shard_map/all_to_all | solution.py:417
  82.8 0.6 shard_map.142
  (25 shorter events, 0.1 us)
Async XLA Ops:
  0.6 10.8 %copy-start.1 = (bf16[512,256]{1,0:T(8,128)(2,1)S(1)}, bf16[512,256]{1,0:T(8,128)(2,1)}, u32[]{:S(2)}) copy-start(bf16[512,256]{1,0:T(8,128)(2,1)} %refs_7_.7) | copy-start | bytes 786436
  0.6 10.8 %copy-start.2 = (bf16[512,256]{1,0:T(8,128)(2,1)S(1)}, bf16[512,256]{1,0:T(8,128)(2,1)}, u32[]{:S(2)}) copy-start(bf16[512,256]{1,0:T(8,128)(2,1)} %refs_4_.7) | copy-start | bytes 786436
  0.7 10.8 %copy-start.3 = (bf16[512,256]{1,0:T(8,128)(2,1)S(1)}, bf16[512,256]{1,0:T(8,128)(2,1)}, u32[]{:S(2)}) copy-start(bf16[512,256]{1,0:T(8,128)(2,1)} %refs_6_.7) | copy-start | bytes 786436
  0.7 10.8 %copy-start.4 = (bf16[512,256]{1,0:T(8,128)(2,1)S(1)}, bf16[512,256]{1,0:T(8,128)(2,1)}, u32[]{:S(2)}) copy-start(bf16[512,256]{1,0:T(8,128)(2,1)} %refs_5_.7) | copy-start | bytes 786436
  0.7 10.8 %copy-start.5 = (bf16[512,16]{0,1:T(8,128)(2,1)S(1)}, bf16[512,16]{0,1:T(8,128)(2,1)}, u32[]{:S(2)}) copy-start(bf16[512,16]{0,1:T(8,128)(2,1)} %param.11) | copy-start | bytes 49156
  0.7 10.8 %copy-start.6 = (bf16[16,256]{1,0:T(8,128)(2,1)S(1)}, bf16[16,256]{1,0:T(8,128)(2,1)}, u32[]{:S(2)}) copy-start(bf16[16,256]{1,0:T(8,128)(2,1)} %refs_9_.1) | copy-start | bytes 24580
  0.7 10.8 %copy-start.7 = (s32[512]{0:T(512)S(1)}, s32[512]{0:T(512)}, u32[]{:S(2)}) copy-start(s32[512]{0:T(512)} %param.14) | copy-start | bytes 6148
  0.7 10.8 %copy-start.8 = (f32[256]{0:T(256)S(1)}, f32[256]{0:T(256)}, u32[]{:S(2)}) copy-start(f32[256]{0:T(256)} %param.13) | copy-start | bytes 3076
  4.3 19.7 %all-to-all-start = ((f32[8,72,128]{2,1,0:T(8,128)}), f32[8,72,128]{2,1,0:T(8,128)S(1)}, u32[]{:S(2)}, u32[]{:S(2)}) async-start(f32[8,72,128]{2,1,0:T(8,128)} %get-tuple-element.25), calls=%async_computation | async-start | bytes 589824 | tf_op jit(solution)/shard_map/all_to_all | solution.py:417
  17.3 1.3 %copy-start.11 = (f32[4,512,256]{2,1,0:T(8,128)}, f32[4,512,256]{2,1,0:T(8,128)S(1)}, u32[]{:S(2)}) copy-start(f32[4,512,256]{2,1,0:T(8,128)S(1)} %get-tuple-element.31.refs_8_) | copy-start | bytes 6291460
  24.1 5.8 %collective-permute-start = (f32[40,128]{1,0:T(8,128)S(1)}, f32[40,128]{1,0:T(8,128)S(1)}, u32[]{:S(2)}, u32[]{:S(2)}) collective-permute-start(f32[40,128]{1,0:T(8,128)S(1)} %get-tuple-element.27), channel_id=1, source_target_pairs={{0,8},{8,16},{16,24},{24,32},{32,40},{40,48},{48,56},{1,9},{9,17},... | collective-permute-start | bytes 61448 | tf_op jit(solution)/shard_map/ppermute | solution.py:423
  28.4 19.1 %copy-start.9 = (f32[2,512,256]{2,1,0:T(8,128)S(1)}, f32[2,512,256]{2,1,0:T(8,128)}, u32[]{:S(2)}) copy-start(f32[2,512,256]{2,1,0:T(8,128)} %get-tuple-element.29.refs_2_) | copy-start | bytes 3145732
  28.4 19.1 %copy-start.10 = (f32[2,2,4,128,128]{4,3,2,1,0:T(8,128)S(1)}, f32[2,2,4,128,128]{4,3,2,1,0:T(8,128)}, u32[]{:S(2)}) copy-start(f32[2,2,4,128,128]{4,3,2,1,0:T(8,128)} %get-tuple-element.30.refs_3_) | copy-start | bytes 3145732
  28.4 6.2 %collective-permute-start.1 = (f32[40,128]{1,0:T(8,128)S(1)}, f32[40,128]{1,0:T(8,128)S(1)}, u32[]{:S(2)}, u32[]{:S(2)}) collective-permute-start(f32[40,128]{1,0:T(8,128)S(1)} %get-tuple-element.28), channel_id=1, source_target_pairs={{8,0},{16,8},{24,16},{32,24},{40,32},{48,40},{56,48},{9,1},{17,9},... | collective-permute-start | bytes 61448 | tf_op jit(solution)/shard_map/ppermute | solution.py:423
  47.5 3.1 %copy-start = (f32[8,64,128]{2,1,0:T(8,128)}, f32[8,64,128]{2,1,0:T(8,128)S(1)}, u32[]{:S(2)}) copy-start(f32[8,64,128]{2,1,0:T(8,128)S(1)} %all_to_all.20.refs_0_) | copy-start | bytes 786436
  50.6 12.8 %all-to-all-start.2 = ((f32[8,40,128]{2,1,0:T(8,128)}), f32[8,40,128]{2,1,0:T(8,128)S(1)}, u32[]{:S(2)}, u32[]{:S(2)}) async-start(f32[8,40,128]{2,1,0:T(8,128)} %get-tuple-element.36), calls=%async_computation.2 | async-start | bytes 327680 | tf_op jit(solution)/shard_map/all_to_all | solution.py:417
  55.8 7.3 %collective-permute-start.2 = (f32[64,128]{1,0:T(8,128)S(1)}, f32[64,128]{1,0:T(8,128)S(1)}, u32[]{:S(2)}, u32[]{:S(2)}) collective-permute-start(f32[64,128]{1,0:T(8,128)S(1)} %reduce_sum.9.lat_ref), channel_id=1, source_target_pairs={{0,256},{128,384},{256,0},{384,128},{1,257},{129,385},{257,1},{385... | collective-permute-start | bytes 98312 | tf_op jit(solution)/shard_map/ppermute | solution.py:427
  64.0 18.8 %all-to-all-start.3 = ((f32[8,40,128]{2,1,0:T(8,128)}), f32[8,40,128]{2,1,0:T(8,128)S(1)}, u32[]{:S(2)}, u32[]{:S(2)}) async-start(f32[8,40,128]{2,1,0:T(8,128)} %get-tuple-element.39), calls=%async_computation.3 | async-start | bytes 327680 | tf_op jit(solution)/shard_map/all_to_all | solution.py:417
  73.4 7.3 %collective-permute-start.3 = (f32[64,128]{1,0:T(8,128)S(1)}, f32[64,128]{1,0:T(8,128)S(1)}, u32[]{:S(2)}, u32[]{:S(2)}) collective-permute-start(f32[64,128]{1,0:T(8,128)S(1)} %get-tuple-element.38.lat_mine_ref), channel_id=1, source_target_pairs={{0,128},{128,0},{256,384},{384,256},{1,129},{129,1},{257,385},{385... | collective-permute-start | bytes 98312 | tf_op jit(solution)/shard_map/ppermute | solution.py:427

commit v3 on v2

--- a/solution.py
+++ b/solution.py
@@ -243,7 +243,7 @@
     sum_ref[: PARTS * RANK, :], sum_ref[PARTS * RANK :, :] = gate_sums(grad_pre, lat_ref, w_ref)
 
 
-def carry(h, seg, gate_ref, state_ref, got_ref):
+def carry(h, seg, gate_ref, state_ref, got_ref, whole=True):
     memory = got_ref[:, h * 16 : (h + 1) * 16, :].reshape(HEAD, HEAD)
     back = got_ref[:, 32 + h * 16 : 48 + h * 16, :].reshape(HEAD, HEAD)
     starts, ends, backs, keeps = [], [], [None] * PARTS, []
@@ -254,8 +254,9 @@
         if c > 0:
             memory = memory * as_number(first == seg[c - 1][3])
         starts.append(memory)
-        memory = state_ref[0, h, c] + keeps[c] * memory
-        ends.append(memory)
+        if whole or c < PARTS - 1:
+            memory = state_ref[0, h, c] + keeps[c] * memory
+            ends.append(memory)
     for c in reversed(range(PARTS)):
         backs[c] = back
         if c > 0:
@@ -306,7 +307,7 @@
     heads = q_ref.shape[1] // HEAD
     need(0, 1, 2, 3)
     seg = [segments(doc_ref, c) for c in range(PARTS)]
-    carried = [carry(h, seg, gate_ref, state_ref, got_ref) for h in range(heads)]
+    carried = [carry(h, seg, gate_ref, state_ref, got_ref, False) for h in range(heads)]
     need(4, 5, 6, 7, 8)
     for c in range(PARTS):
         at = chunk(c)
@@ -353,21 +354,23 @@
     return pl.CostEstimate(flops=flops, bytes_accessed=moved, transcendentals=0)
 
 
-def call(kernel, outs, *operands):
+def call(kernel, outs, *operands, flops=10**10):
     return pl.pallas_call(
         kernel,
         out_shape=outs,
         in_specs=[pl.BlockSpec(memory_space=pltpu.VMEM)] * len(operands),
         out_specs=jax.tree.map(lambda _: pl.BlockSpec(memory_space=pltpu.VMEM), outs),
-        cost_estimate=estimate(operands, 10**10),
+        cost_estimate=estimate(operands, flops),
         compiler_params=pltpu.CompilerParams(vmem_limit_bytes=16 * 2**20),
     )(*operands)
 
 
-def call_streamed(kernel, outs, *operands, flops, read=True, write=None, limit=60):
+def call_streamed(kernel, outs, *operands, flops, read=True, write=None, limit=60, taken=None):
     n, m = len(operands), len(outs)
     pieces = 16
     write = tuple(range(m)) if write is None else write
+    taken = [(taken or {}).get(i, [slice(None)]) for i in range(n)]
+    first = [sum(map(len, taken[:i])) for i in range(n + 1)]
 
     def run(*refs):
         sources, results, refs = refs[:n], refs[n : n + m], refs[n + m :]
@@ -376,14 +379,22 @@
         for i, buffer in zip(write, refs, strict=False):
             held[i] = buffer
         arrived, sent = refs[-2:]
-        copies = [pltpu.make_async_copy(sources[i], ins[i], arrived.at[i]) for i in range(n)] if read else []
-        for copy in copies:
-            copy.start()
+        copies = [
+            [
+                pltpu.make_async_copy(sources[i].at[at], ins[i].at[at], arrived.at[first[i] + j])
+                for j, at in enumerate(taken[i])
+            ]
+            for i in (range(n) if read else ())
+        ]
+        for group in copies:
+            for copy in group:
+                copy.start()
         going = []
 
         def need(*which):
             for i in which if read else ():
-                copies[i].wait()
+                for copy in copies[i]:
+                    copy.wait()
 
         def emit(i, at):
             if i in write:
@@ -403,7 +414,7 @@
         out_shape=outs,
         in_specs=[pl.BlockSpec(memory_space=spaces[read])] * n,
         out_specs=tuple(pl.BlockSpec(memory_space=spaces[i in write]) for i in range(m)),
-        scratch_shapes=[*buffers, pltpu.SemaphoreType.DMA((n,)), pltpu.SemaphoreType.DMA((pieces,))],
+        scratch_shapes=[*buffers, pltpu.SemaphoreType.DMA((first[n],)), pltpu.SemaphoreType.DMA((pieces,))],
         cost_estimate=estimate(operands, flops),
         compiler_params=pltpu.CompilerParams(vmem_limit_bytes=limit * 2**20),
     )(*operands)
@@ -444,7 +455,7 @@
     )
     terms, sums = call_streamed(
         inner_kernel, (shape((4, tokens, width)), shape((PARTS * RANK + 40, HEAD))),
-        *operands, flops=INNER_FLOPS, read=False, write=(0,), limit=INNER_HELD,
+        *operands, flops=INNER_FLOPS, read=False, write=(), limit=INNER_HELD,
     )
     got = exchange(send, "y")
     ahead, behind = call(total_kernel, (shape((40, HEAD)), shape((40, HEAD))), got, sums)
@@ -456,15 +467,17 @@
         flops=2 * 10**9, read=False, write=(), limit=HELD,
     )
     results = call_streamed(
-        outer_kernel, (half, half, half, half), *common, terms, flops=3 * 10**9
+        outer_kernel, (half, half, half, half), *common, terms,
+        flops=3 * 10**9, taken={2: [0], 3: [(0, slice(None), slice(0, 3)), (1, slice(None), slice(1, 4))]},
     )
     w_got = exchange(w_send, "y")
     lat_send = jnp.sum(lax.all_gather(lat_send, "core"), axis=0)
     w_send, lat_send = call(
-        resend_kernel, (ring, lat_shape), w_got, lat_send, swapped(lat_send, "x", 2)
+        resend_kernel, (ring, lat_shape), w_got, lat_send, swapped(lat_send, "x", 1),
+        flops=10**11,
     )
     w_got = exchange(w_send, "z")
-    lat_got = swapped(lat_send, "x", 1)
+    lat_got = swapped(lat_send, "x", 2)
     grad_lat, grad_w, grad_b = call(
         finish_kernel, (shape((RANK, tokens)), shape((RANK, width)), shape((1, width))),
         lat_send, lat_got, w_got,

time: 84.1 us -> 84 us (level)
  Pallas kernels: 18.4 us -> 17.4 us
  waiting for transfers between devices: 16.4 us -> 17.4 us
    all_to_all x3, waiting for transfers between devices: 7.69 us -> 9.61 us  [exchange(): return lax.all_to_all(x, axis, 0, 0)]
    pallas_call x4, Pallas kernels: 17 us -> 16 us  [call_streamed(): pl.pallas_call(run, out_shape=outs, in_specs=[pl.BlockSpec(memory_space=s...]
    ppermute x2, waiting for transfers between devices: 3.99 us -> 3.06 us  [swapped(): lax.ppermute(value, axis, [(s, s ^ bit) for s in range(lax.axis_size(axis...]
  transfers between devices with their start and end apart: 7 -> 7, of which waited for: 5 -> 5; matrix products, arithmetic and copies ran while one was open for 0% -> 0% of each run, Pallas kernels for 12% -> 11%
where the time goes in v3:
time: 84 us; the launch traced here: 83.4 us
  starting transfers between devices  31.6 us (38%)
  Pallas kernels  17.4 us (21%)
  waiting for transfers between devices  17.4 us (21%)
  blocking collectives  14.7 us (18%)
  local copies, waits for them, and re-layouts  1.38 us (2%)
  between operations  0.88 us (1%)
    all_to_all x3, starting transfers between devices, exchange(): return lax.all_to_all(x, axis, 0, 0)  19.9 us
    pallas_call x4, Pallas kernels, call_streamed(): pl.pallas_call(run, out_shape=outs, in_specs=[pl.BlockSpec(memory_space=s...  16 us
    all_to_all x1, blocking collectives, exchange(): return lax.all_to_all(x, axis, 0, 0)  12.9 us
    all_to_all x3, waiting for transfers between devices, exchange(): return lax.all_to_all(x, axis, 0, 0)  9.61 us
    ppermute x2, starting transfers between devices, swapped(): lax.ppermute(value, axis, [(s, s ^ bit) for s in range(lax.axis_size(axis...  6.04 us
    ppermute x2, starting transfers between devices, passed(): return lax.ppermute(value, axis, pairs)  5.71 us
    ppermute x2, waiting for transfers between devices, passed(): return lax.ppermute(value, axis, pairs)  4.73 us
    ppermute x2, waiting for transfers between devices, swapped(): lax.ppermute(value, axis, [(s, s ^ bit) for s in range(lax.axis_size(axis...  3.06 us
  transfers between devices with their start and end apart: 7, of which 5 were waited for; matrix products, arithmetic and copies ran while one was open for 0% of the time, Pallas kernels for 11%

profile of v3, /device:TPU:6, one launch (start us, length us, event | category | flops | bytes accessed | tf_op | source)
XLA Modules:
  0.0 83.4 jit_solution(15888367118282764091)
XLA Ops:
  0.6 0.0 copy-start.1
  0.7 0.0 copy-start.4
  0.7 3.6 %shard_map.135 = (f32[8,72,128]{2,1,0:T(8,128)}, f32[2,512,256]{2,1,0:T(8,128)}, f32[2,2,4,128,128]{4,3,2,1,0:T(8,128)}) custom-call(bf16[16,512]{1,0:T(8,128)(2,1)} %bitcast.6, bf16[16,256]{1,0:T(8,128)(2,1)} %refs_9_.1, f32[1,256]{1,0:T(1,128)} %bitcast.13, s32[4,128]{1,0:T(4,128)} %bitcast.9, bf16[512,256]{1,0:T(8,128)(2,1)} %refs_7_.7, ...), custom_call_target="tpu_custom_call" | custom-call | flops 1000000000 | bytes 1076224 | tf_op jit(solution)/shard_map/pallas_call | solution.py:412
  4.3 7.1 %all-to-all-start = ((f32[8,72,128]{2,1,0:T(8,128)}), f32[8,72,128]{2,1,0:T(8,128)S(1)}, u32[]{:S(2)}, u32[]{:S(2)}) async-start(f32[8,72,128]{2,1,0:T(8,128)} %get-tuple-element.25), calls=%async_computation | async-start | bytes 589824 | tf_op jit(solution)/shard_map/all_to_all | solution.py:428
  11.5 5.0 %shard_map.136 = (f32[4,512,256]{2,1,0:T(8,128)S(1)}, f32[104,128]{1,0:T(8,128)S(1)}) custom-call(bf16[16,512]{1,0:T(8,128)(2,1)S(1)} %bitcast.7, bf16[16,256]{1,0:T(8,128)(2,1)S(1)} %copy-done.6, f32[1,256]{1,0:T(1,128)S(1)} %bitcast.14, s32[4,128]{1,0:T(4,128)S(1)} %bitcast.11, bf16[512,256]{1,0:T(8,128)(2,1)S(1)} %copy-done.1, ...), custom_call_target="tpu_custom_call" | custom-call | flops 40000000000 | bytes 1076224 | tf_op jit(solution)/shard_map/pallas_call | solution.py:412
  16.5 1.3 %copy-done.11 = f32[4,512,256]{2,1,0:T(8,128)} copy-done((f32[4,512,256]{2,1,0:T(8,128)}, f32[4,512,256]{2,1,0:T(8,128)S(1)}, u32[]{:S(2)}) %copy-start.11) | copy-done | bytes 2097176
  17.9 6.2 %all-to-all-done.got_ref = f32[8,72,128]{2,1,0:T(8,128)S(1)} async-done(((f32[8,72,128]{2,1,0:T(8,128)}), f32[8,72,128]{2,1,0:T(8,128)S(1)}, u32[]{:S(2)}, u32[]{:S(2)}) %all-to-all-start) | async-done | bytes 294944 | tf_op jit(solution)/shard_map/all_to_all | solution.py:428
  24.1 4.3 %collective-permute-start = (f32[40,128]{1,0:T(8,128)S(1)}, f32[40,128]{1,0:T(8,128)S(1)}, u32[]{:S(2)}, u32[]{:S(2)}) collective-permute-start(f32[40,128]{1,0:T(8,128)S(1)} %get-tuple-element.27), channel_id=1, source_target_pairs={{0,8},{8,16},{16,24},{24,32},{32,40},{40,48},{48,56},{1,9},{9,17},... | collective-permute-start | bytes 61448 | tf_op jit(solution)/shard_map/ppermute | solution.py:434
  28.4 1.4 %collective-permute-start.1 = (f32[40,128]{1,0:T(8,128)S(1)}, f32[40,128]{1,0:T(8,128)S(1)}, u32[]{:S(2)}, u32[]{:S(2)}) collective-permute-start(f32[40,128]{1,0:T(8,128)S(1)} %get-tuple-element.28), channel_id=1, source_target_pairs={{8,0},{16,8},{24,16},{32,24},{40,32},{48,40},{56,48},{9,1},{17,9},... | collective-permute-start | bytes 61448 | tf_op jit(solution)/shard_map/ppermute | solution.py:434
  29.8 0.0 collective-permute-done.ahead_ref
  29.8 4.7 %collective-permute-done.1.behind_ref = f32[40,128]{1,0:T(8,128)S(1)} collective-permute-done((f32[40,128]{1,0:T(8,128)S(1)}, f32[40,128]{1,0:T(8,128)S(1)}, u32[]{:S(2)}, u32[]{:S(2)}) %collective-permute-start.1) | collective-permute-done | bytes 20512 | tf_op jit(solution)/shard_map/ppermute | solution.py:434
  34.6 12.9 %all_to_all.20.refs_0_ = f32[8,64,128]{2,1,0:T(8,128)S(1)} all-to-all(f32[8,64,128]{2,1,0:T(8,128)S(1)} %shard_map.138), channel_id=1, replica_groups=mesh['x'=4,'core'=2,'z'=8,'y'=8] {'y'}, dimensions={0} | all-to-all | bytes 524288 | tf_op jit(solution)/shard_map/all_to_all | solution.py:428
  47.5 3.1 %shard_map.140 = (f32[64,128]{1,0:T(8,128)S(1)}, f32[8,40,128]{2,1,0:T(8,128)}) custom-call(f32[8,64,128]{2,1,0:T(8,128)S(1)} %all_to_all.20.refs_0_, s32[4,128]{1,0:T(4,128)S(1)} %bitcast.12, f32[2,512,256]{2,1,0:T(8,128)S(1)} %copy-done.9, f32[2,2,4,128,128]{4,3,2,1,0:T(8,128)S(1)} %copy-done.10, bf16[512,256]{1,0:T(8,128)(2,1)S(1)} %copy-done.2, ...), custom_call_target="tpu_custom_call" | custom-call | flops 2000000000 | bytes 3487744 | tf_op jit(solution)/shard_map/pallas_call | solution.py:412
  50.6 3.4 %all-to-all-start.2 = ((f32[8,40,128]{2,1,0:T(8,128)}), f32[8,40,128]{2,1,0:T(8,128)S(1)}, u32[]{:S(2)}, u32[]{:S(2)}) async-start(f32[8,40,128]{2,1,0:T(8,128)} %get-tuple-element.36), calls=%async_computation.2 | async-start | bytes 327680 | tf_op jit(solution)/shard_map/all_to_all | solution.py:428
  54.0 1.9 %all-gather = f32[128,128]{1,0:T(8,128)S(1)} all-gather(f32[64,128]{1,0:T(8,128)S(1)} %get-tuple-element.37), channel_id=2, replica_groups=mesh['x'=4,'core'=2,'z'=8,'y'=8] {'core'}, dimensions={0}, use_global_device_ids=true | all-gather | bytes 98304 | tf_op jit(solution)/shard_map/all_gather | solution.py:474
  55.8 2.7 %collective-permute-start.2 = (f32[64,128]{1,0:T(8,128)S(1)}, f32[64,128]{1,0:T(8,128)S(1)}, u32[]{:S(2)}, u32[]{:S(2)}) collective-permute-start(f32[64,128]{1,0:T(8,128)S(1)} %reduce_sum.9.lat_ref), channel_id=1, source_target_pairs={{0,128},{128,0},{256,384},{384,256},{1,129},{129,1},{257,385},{385... | collective-permute-start | bytes 98312 | tf_op jit(solution)/shard_map/ppermute | solution.py:438
  58.6 3.1 %collective-permute-done.2.lat_got_ref = f32[64,128]{1,0:T(8,128)S(1)} collective-permute-done((f32[64,128]{1,0:T(8,128)S(1)}, f32[64,128]{1,0:T(8,128)S(1)}, u32[]{:S(2)}, u32[]{:S(2)}) %collective-permute-start.2) | collective-permute-done | bytes 32800 | tf_op jit(solution)/shard_map/ppermute | solution.py:438
  61.6 1.7 %all-to-all-done.2.got_ref = f32[8,40,128]{2,1,0:T(8,128)S(1)} async-done(((f32[8,40,128]{2,1,0:T(8,128)}), f32[8,40,128]{2,1,0:T(8,128)S(1)}, u32[]{:S(2)}, u32[]{:S(2)}) %all-to-all-start.2) | async-done | bytes 163872 | tf_op jit(solution)/shard_map/all_to_all | solution.py:428
  63.3 0.7 shard_map.141
  64.0 9.3 %all-to-all-start.3 = ((f32[8,40,128]{2,1,0:T(8,128)}), f32[8,40,128]{2,1,0:T(8,128)S(1)}, u32[]{:S(2)}, u32[]{:S(2)}) async-start(f32[8,40,128]{2,1,0:T(8,128)} %get-tuple-element.39), calls=%async_computation.3 | async-start | bytes 327680 | tf_op jit(solution)/shard_map/all_to_all | solution.py:428
  73.4 3.3 %collective-permute-start.3 = (f32[64,128]{1,0:T(8,128)S(1)}, f32[64,128]{1,0:T(8,128)S(1)}, u32[]{:S(2)}, u32[]{:S(2)}) collective-permute-start(f32[64,128]{1,0:T(8,128)S(1)} %get-tuple-element.38.lat_mine_ref), channel_id=1, source_target_pairs={{0,256},{128,384},{256,0},{384,128},{1,257},{129,385},{257,1},{385... | collective-permute-start | bytes 98312 | tf_op jit(solution)/shard_map/ppermute | solution.py:438
  76.7 4.3 %shard_map.139 = (bf16[512,256]{1,0:T(8,128)(2,1)}, bf16[512,256]{1,0:T(8,128)(2,1)}, bf16[512,256]{1,0:T(8,128)(2,1)}, bf16[512,256]{1,0:T(8,128)(2,1)}) custom-call(f32[8,64,128]{2,1,0:T(8,128)} %copy-done, s32[4,128]{1,0:T(4,128)} %bitcast.10, f32[2,512,256]{2,1,0:T(8,128)} %get-tuple-element.29.refs_2_, ...), custom_call_target="tpu_custom_call" | custom-call | flops 3000000000 | bytes 5507072 | tf_op jit(solution)/shard_map/pallas_call | solution.py:412
  81.0 1.8 %all-to-all-done.3.w_got_ref = f32[8,40,128]{2,1,0:T(8,128)S(1)} async-done(((f32[8,40,128]{2,1,0:T(8,128)}), f32[8,40,128]{2,1,0:T(8,128)S(1)}, u32[]{:S(2)}, u32[]{:S(2)}) %all-to-all-start.3) | async-done | bytes 163872 | tf_op jit(solution)/shard_map/all_to_all | solution.py:428
  82.8 0.6 shard_map.142
  (25 shorter events, 0.1 us)
Async XLA Ops:
  0.6 10.8 %copy-start.1 = (bf16[512,256]{1,0:T(8,128)(2,1)S(1)}, bf16[512,256]{1,0:T(8,128)(2,1)}, u32[]{:S(2)}) copy-start(bf16[512,256]{1,0:T(8,128)(2,1)} %refs_7_.7) | copy-start | bytes 786436
  0.6 10.8 %copy-start.2 = (bf16[512,256]{1,0:T(8,128)(2,1)S(1)}, bf16[512,256]{1,0:T(8,128)(2,1)}, u32[]{:S(2)}) copy-start(bf16[512,256]{1,0:T(8,128)(2,1)} %refs_4_.7) | copy-start | bytes 786436
  0.7 10.8 %copy-start.3 = (bf16[512,256]{1,0:T(8,128)(2,1)S(1)}, bf16[512,256]{1,0:T(8,128)(2,1)}, u32[]{:S(2)}) copy-start(bf16[512,256]{1,0:T(8,128)(2,1)} %refs_6_.7) | copy-start | bytes 786436
  0.7 10.8 %copy-start.4 = (bf16[512,256]{1,0:T(8,128)(2,1)S(1)}, bf16[512,256]{1,0:T(8,128)(2,1)}, u32[]{:S(2)}) copy-start(bf16[512,256]{1,0:T(8,128)(2,1)} %refs_5_.7) | copy-start | bytes 786436
  0.7 10.8 %copy-start.5 = (bf16[512,16]{0,1:T(8,128)(2,1)S(1)}, bf16[512,16]{0,1:T(8,128)(2,1)}, u32[]{:S(2)}) copy-start(bf16[512,16]{0,1:T(8,128)(2,1)} %param.11) | copy-start | bytes 49156
  0.7 10.8 %copy-start.6 = (bf16[16,256]{1,0:T(8,128)(2,1)S(1)}, bf16[16,256]{1,0:T(8,128)(2,1)}, u32[]{:S(2)}) copy-start(bf16[16,256]{1,0:T(8,128)(2,1)} %refs_9_.1) | copy-start | bytes 24580
  0.7 10.8 %copy-start.7 = (s32[512]{0:T(512)S(1)}, s32[512]{0:T(512)}, u32[]{:S(2)}) copy-start(s32[512]{0:T(512)} %param.14) | copy-start | bytes 6148
  0.7 10.8 %copy-start.8 = (f32[256]{0:T(256)S(1)}, f32[256]{0:T(256)}, u32[]{:S(2)}) copy-start(f32[256]{0:T(256)} %param.13) | copy-start | bytes 3076
  4.3 19.7 %all-to-all-start = ((f32[8,72,128]{2,1,0:T(8,128)}), f32[8,72,128]{2,1,0:T(8,128)S(1)}, u32[]{:S(2)}, u32[]{:S(2)}) async-start(f32[8,72,128]{2,1,0:T(8,128)} %get-tuple-element.25), calls=%async_computation | async-start | bytes 589824 | tf_op jit(solution)/shard_map/all_to_all | solution.py:428
  16.5 1.3 %copy-start.11 = (f32[4,512,256]{2,1,0:T(8,128)}, f32[4,512,256]{2,1,0:T(8,128)S(1)}, u32[]{:S(2)}) copy-start(f32[4,512,256]{2,1,0:T(8,128)S(1)} %get-tuple-element.31.refs_8_) | copy-start | bytes 6291460
  24.1 5.8 %collective-permute-start = (f32[40,128]{1,0:T(8,128)S(1)}, f32[40,128]{1,0:T(8,128)S(1)}, u32[]{:S(2)}, u32[]{:S(2)}) collective-permute-start(f32[40,128]{1,0:T(8,128)S(1)} %get-tuple-element.27), channel_id=1, source_target_pairs={{0,8},{8,16},{16,24},{24,32},{32,40},{40,48},{48,56},{1,9},{9,17},... | collective-permute-start | bytes 61448 | tf_op jit(solution)/shard_map/ppermute | solution.py:434
  28.4 19.1 %copy-start.9 = (f32[2,512,256]{2,1,0:T(8,128)S(1)}, f32[2,512,256]{2,1,0:T(8,128)}, u32[]{:S(2)}) copy-start(f32[2,512,256]{2,1,0:T(8,128)} %get-tuple-element.29.refs_2_) | copy-start | bytes 3145732
  28.4 19.1 %copy-start.10 = (f32[2,2,4,128,128]{4,3,2,1,0:T(8,128)S(1)}, f32[2,2,4,128,128]{4,3,2,1,0:T(8,128)}, u32[]{:S(2)}) copy-start(f32[2,2,4,128,128]{4,3,2,1,0:T(8,128)} %get-tuple-element.30.refs_3_) | copy-start | bytes 3145732
  28.4 6.2 %collective-permute-start.1 = (f32[40,128]{1,0:T(8,128)S(1)}, f32[40,128]{1,0:T(8,128)S(1)}, u32[]{:S(2)}, u32[]{:S(2)}) collective-permute-start(f32[40,128]{1,0:T(8,128)S(1)} %get-tuple-element.28), channel_id=1, source_target_pairs={{8,0},{16,8},{24,16},{32,24},{40,32},{48,40},{56,48},{9,1},{17,9},... | collective-permute-start | bytes 61448 | tf_op jit(solution)/shard_map/ppermute | solution.py:434
  47.5 3.1 %copy-start = (f32[8,64,128]{2,1,0:T(8,128)}, f32[8,64,128]{2,1,0:T(8,128)S(1)}, u32[]{:S(2)}) copy-start(f32[8,64,128]{2,1,0:T(8,128)S(1)} %all_to_all.20.refs_0_) | copy-start | bytes 786436
  50.6 12.8 %all-to-all-start.2 = ((f32[8,40,128]{2,1,0:T(8,128)}), f32[8,40,128]{2,1,0:T(8,128)S(1)}, u32[]{:S(2)}, u32[]{:S(2)}) async-start(f32[8,40,128]{2,1,0:T(8,128)} %get-tuple-element.36), calls=%async_computation.2 | async-start | bytes 327680 | tf_op jit(solution)/shard_map/all_to_all | solution.py:428
  55.8 5.8 %collective-permute-start.2 = (f32[64,128]{1,0:T(8,128)S(1)}, f32[64,128]{1,0:T(8,128)S(1)}, u32[]{:S(2)}, u32[]{:S(2)}) collective-permute-start(f32[64,128]{1,0:T(8,128)S(1)} %reduce_sum.9.lat_ref), channel_id=1, source_target_pairs={{0,128},{128,0},{256,384},{384,256},{1,129},{129,1},{257,385},{385... | collective-permute-start | bytes 98312 | tf_op jit(solution)/shard_map/ppermute | solution.py:438
  64.0 18.8 %all-to-all-start.3 = ((f32[8,40,128]{2,1,0:T(8,128)}), f32[8,40,128]{2,1,0:T(8,128)S(1)}, u32[]{:S(2)}, u32[]{:S(2)}) async-start(f32[8,40,128]{2,1,0:T(8,128)} %get-tuple-element.39), calls=%async_computation.3 | async-start | bytes 327680 | tf_op jit(solution)/shard_map/all_to_all | solution.py:428
  73.4 7.7 %collective-permute-start.3 = (f32[64,128]{1,0:T(8,128)S(1)}, f32[64,128]{1,0:T(8,128)S(1)}, u32[]{:S(2)}, u32[]{:S(2)}) collective-permute-start(f32[64,128]{1,0:T(8,128)S(1)} %get-tuple-element.38.lat_mine_ref), channel_id=1, source_target_pairs={{0,256},{128,384},{256,0},{384,128},{1,257},{129,385},{257,1},{385... | collective-permute-start | bytes 98312 | tf_op jit(solution)/shard_map/ppermute | solution.py:438
